TPU v7x, 512 devices: a whole 4x8x8 slice. The times are simulated.
512 devices in a mesh: row: 64 (over x, z, core), col: 8 (over y).
Axes of the slice: x: 4, y: 8, z: 8, core: 2. Of those that a mesh axis runs over, the one named last changes fastest.
Arguments:
- features: bfloat16 [262144, 512], P(('row', 'col')), may hold values from -6 to 6
- factor: float32 [262144, 1024], P(('row', 'col')), may hold values from -0.03 to 0.03
- ip_weights: float32 [262144], P(('row', 'col')), may hold values from 0.1 to 30
- pivot_owner: int32 [256], replicated, may hold values from 0 to 511, as said below
- pivot_position: int32 [256], replicated, may hold values from 0 to 511, as said below
Outputs:
- new_columns: float32 [262144, 256], P(('row', 'col'))
- gram_rows: float32 [256, 1280], replicated
Inputs may be any that keep to these rules, and one draw needn't show every extreme that they name: `pivot_owner`: each device owns at most 3 pivots, and some device owns exactly 3. `pivot_position`: pivots with the same owner have different positions.
All inputs are finite; a program needn't handle non-finite values.
Results may differ from a plain program's by a relative error of at most 0.0003.
Values may be sent and summed in bfloat16 or wider, within the bound.
A program may use at most 64 MiB of HBM per device.

v0:
```python
import jax
import jax.numpy as jnp
from jax import lax
from jax.sharding import Mesh
from jax.sharding import PartitionSpec as P

F = 512
ROW = ("row_0", "row_1", "row_2")
ROW_COL = ("row_0", "row_1", "row_2", "col")


kernel_rates = (0.25, 0.5, 1.0)
kernel_mixes = (0.5, 0.3, 0.2)


def copy_for_each(array, axis):
    copies = jnp.broadcast_to(array, (lax.axis_size(axis), *array.shape))
    return lax.all_to_all(copies, axis, split_axis=0, concat_axis=0, tiled=True)


def in_order(parts, dim):
    dims = list(parts.shape[1:])
    dims[dim] *= parts.shape[0]
    return jnp.moveaxis(parts, 0, dim).reshape(dims)


def gather_axes(array, axes, dim):
    far, near = axes
    parts = copy_for_each(copy_for_each(array, far), near)
    return in_order(parts.swapaxes(0, 1).reshape(-1, *array.shape), dim)


def cut_along(array, dim, length):
    before, after = (array.shape[:dim], array.shape[dim + 1 :])
    return jnp.moveaxis(array.reshape(*before, length, -1, *after), dim, 0)


def summed_on_arrival(array, axis, dim):
    parts = cut_along(array, dim, lax.axis_size(axis))
    arrived = lax.all_to_all(parts, axis, split_axis=0, concat_axis=0, tiled=True)
    return arrived.sum(axis=0)


def sum_by_axis(array, axes, dim):
    far, near = axes
    own = summed_on_arrival(cut_along(array, dim, lax.axis_size(far)), near, dim + 1)
    return jnp.sum(lax.all_to_all(own, far, 0, 0, tiled=True), axis=0)


def rows_for(lines, length):
    spare = -lines.shape[0] % length
    if not spare:
        return lines
    return jnp.concatenate([lines, jnp.zeros((spare, *lines.shape[1:]), lines.dtype)])


def total_of(array, axes):
    lines = array.reshape(-1)
    own = sum_by_axis(rows_for(lines, lax.axis_size(axes[0]) * lax.axis_size(axes[1])), axes, 0)
    whole = gather_axes(own, axes, 0)
    return whole[: len(lines)].reshape(array.shape)


def kernel_of(left, right):
    cross_term = jnp.dot(left, right.T, preferred_element_type=jnp.float32)
    left_norms = jnp.sum(jnp.square(left.astype(jnp.float32)), axis=1)
    right_norms = jnp.sum(jnp.square(right.astype(jnp.float32)), axis=1)
    distance = left_norms[:, None] + right_norms[None, :] - 2.0 * cross_term
    total = jnp.zeros_like(distance)
    for rate, mixing in zip(kernel_rates, kernel_mixes):
        total = total + mixing * jnp.exp(-(rate / F) * distance)
    return total


def body(features, factor, ip_weights, pivot_owner, pivot_position):
    devices = lax.axis_size(ROW) * lax.axis_size("col")
    device_rank = lax.axis_index(ROW) * lax.axis_size("col") + lax.axis_index("col")
    pivot_count = pivot_owner.shape[0]
    slot_count = 2 * pivot_count // devices + 2
    same_owner = pivot_owner[:, None] == pivot_owner[None, :]
    earlier = jnp.arange(pivot_count)[None, :] < jnp.arange(pivot_count)[:, None]
    slot_rank = jnp.sum((same_owner & earlier).astype(jnp.int32), axis=1)
    chosen = (pivot_owner == device_rank)[None, :] & (
        slot_rank[None, :] == jnp.arange(slot_count)[:, None]
    )
    filled = jnp.any(chosen, axis=1)[:, None]
    slot_rows = jnp.sum(jnp.where(chosen, pivot_position[None, :], 0), axis=1)
    slot_x = jnp.where(filled, features[slot_rows], jnp.zeros((), jnp.bfloat16))
    slot_h = jnp.where(filled, factor[slot_rows], 0.0)
    every_x = gather_axes(slot_x, (("row_0", "row_1"), ("row_2", "col")), 0)
    every_h = lax.all_gather(slot_h, ROW_COL, axis=0, tiled=True)
    source = pivot_owner * slot_count + slot_rank
    pivot_x = every_x[source]
    pivot_h = every_h[source]
    residual = kernel_of(features, pivot_x) - jnp.dot(
        factor, pivot_h.T, precision=lax.Precision.HIGHEST
    )
    block = kernel_of(pivot_x, pivot_x) - jnp.dot(
        pivot_h, pivot_h.T, precision=lax.Precision.HIGHEST
    )
    lower_block = jnp.linalg.cholesky(block)
    new_columns = jax.scipy.linalg.solve_triangular(lower_block, residual.T, lower=True).T
    weighted = new_columns * ip_weights[:, None]
    left_part = jnp.dot(weighted.T, factor, precision=lax.Precision.HIGHEST)
    right_part = jnp.dot(weighted.T, new_columns, precision=lax.Precision.HIGHEST)
    local_gram = jnp.concatenate([left_part, right_part], axis=1)
    summed = total_of(local_gram, (("row_0", "row_1"), ("row_2", "col")))
    total_samples = features.shape[0] * devices
    return (new_columns, summed / total_samples)


def solution(mesh):
    torus = Mesh(
        mesh.devices.reshape(4, 8, 2, mesh.shape["col"]), ("row_0", "row_1", "row_2", "col")
    )
    in_specs = (P(ROW_COL, None), P(ROW_COL, None), P(ROW_COL), P(), P())
    out_specs = (P(ROW_COL, None), P())
    return jax.shard_map(body, mesh=torus, in_specs=in_specs, out_specs=out_specs, check_vma=False)
```

profile of v0, /device:TPU:1, one launch (start us, length us, event | category | flops | bytes accessed | tf_op | source)
XLA Modules:
  0.0 362.9 jit_solution(6088916679859474437)
XLA Ops:
  7.2 1.0 convert_reduce_fusion
  8.2 0.7 broadcast_compare_fusion
  9.1 0.8 select_reduce_fusion.2
  9.9 0.6 gather_fusion.2
  10.4 0.7 select_bitcast_fusion.1
  11.2 1.7 gather_fusion
  13.0 22.7 %all_to_all.38 = bf16[32,3,512]{2,1,0:T(4,128)(2,1)S(1)} all-to-all(bf16[32,3,512]{2,1,0:T(4,128)(2,1)S(1)} %broadcast_in_dim.74), channel_id=1, replica_groups=mesh['row_0'=4,'row_1'=8,'row_2'=2,'col'=8] {'row_0','row_1'}, dimensions={0} | all-to-all | bytes 196608 | tf_op jit(solution)/shard_map/all_to_all | solution.py:18
  35.6 1.4 broadcast_in_dim.75
  37.1 9.3 %all-to-all-start.1 = ((bf16[16,32,3,512]{3,1,2,0:T(8,128)(2,1)}), bf16[16,32,3,512]{3,1,2,0:T(8,128)(2,1)}, u32[]{:S(2)}, u32[]{:S(2)}) async-start(bf16[16,32,3,512]{3,1,2,0:T(8,128)(2,1)} %broadcast_in_dim.75), calls=%async_computation.1 | async-start | bytes 3145728 | tf_op jit(solution)/shard_map/all_to_all | solution.py:18
  46.6 37.9 %all-to-all-done.1 = bf16[16,32,3,512]{3,1,2,0:T(8,128)(2,1)} async-done(((bf16[16,32,3,512]{3,1,2,0:T(8,128)(2,1)}), bf16[16,32,3,512]{3,1,2,0:T(8,128)(2,1)}, u32[]{:S(2)}, u32[]{:S(2)}) %all-to-all-start.1) | async-done | bytes 1572896 | tf_op jit(solution)/shard_map/all_to_all | solution.py:18
  84.5 4.2 %copy.42 = bf16[32,16,3,512]{3,2,1,0:T(4,128)(2,1)} copy(bf16[32,16,3,512]{3,0,2,1:T(8,128)(2,1)} %bitcast.2) | data formatting | bytes 3145728 | tf_op jit(solution)/shard_map/transpose | solution.py:30
  88.6 5.1 %reshape_reshape.3 = bf16[1536,512]{1,0:T(8,128)(2,1)} reshape(bf16[32,16,3,512]{3,2,1,0:T(4,128)(2,1)} %copy.42) | data formatting | bytes 3145728 | tf_op jit(solution)/shard_map/reshape;reshape | solution.py:24
  93.7 2.8 gather_fusion.1
  96.8 0.8 copy.44
  97.8 1.1 fusion
  98.9 55.2 %all-gather.3.cloned.1.call-done = f32[512,3,1024]{2,1,0:T(4,128)} async-done(((f32[1,3,1024]{2,1,0:T(4,128)}), f32[512,3,1024]{2,1,0:T(4,128)}) %all-gather.3.cloned.1.call-update) | async-done | bytes 6291472 | tf_op jit(solution)/shard_map/all_gather | solution.py:91
  154.1 10.8 %reshape.108 = f32[1536,1024]{1,0:T(8,128)} reshape(f32[512,3,1024]{2,1,0:T(4,128)} %all-gather.3.cloned.1.call-done) | data formatting | bytes 12582912
  164.9 4.4 %gather_fusion.3 = f32[256,1024]{1,0:T(8,128)S(1)} fusion(f32[1536,1024]{1,0:T(8,128)} %reshape.108, s32[1024]{0:T(1024)S(1)} %pad_clamp_fusion), kind=kCustom, calls=%fused_computation.3 | custom fusion | bytes 2098176 | tf_op jit(solution)/shard_map/gather | solution.py:94
  169.3 1.7 fusion.26
  171.0 2.9 convolution_subtract_fusion
  173.9 1.1 copy.45
  174.9 1.4 fusion.9
  176.4 11.7 %cholesky.50 = f32[128,128]{1,0:T(8,128)S(1)} custom-call(f32[128,128]{1,0:T(8,128)S(1)} %cholesky.118), custom_call_target="Cholesky" | custom-call | tf_op jit(solution)/shard_map/jit(cholesky)/cholesky | solution.py:101
  188.2 9.8 %custom-call.15 = f32[1,128,128]{1,2,0:T(8,128)S(1)} custom-call(f32[1,128,128]{2,1,0:T(8,128)S(1)} %get-tuple-element.35), custom_call_target="InvertDiagBlocksLowerTriangular" | custom-call | tf_op jit(solution)/shard_map/jit(cholesky)/cholesky | solution.py:101
  198.4 11.9 %cholesky.105 = f32[128,128]{1,0:T(8,128)S(1)} custom-call(f32[128,128]{1,0:T(8,128)S(1)} %convolution_subtract_fusion.2), custom_call_target="Cholesky" | custom-call | tf_op jit(solution)/shard_map/jit(cholesky)/cholesky | solution.py:101
  210.4 0.7 compare_reduce_fusion
  212.6 4.1 %while.1 = (s32[]{:T(128)}, f32[256,256]{1,0:T(8,128)S(1)}, s32[2,2]{1,0:T(2,128)S(1)}, f32[2,128,128]{2,1,0:T(8,128)S(1)}, s32[]{:T(128)}) while((s32[]{:T(128)}, f32[256,256]{1,0:T(8,128)S(1)}, s32[2,2]{1,0:T(2,128)S(1)}, f32[2,128,128]{2,1,0:T(8,128)S(1)}, s32[]{:T(128)}) %tuple.33), condition=%wide.while_cond, body=%wide.while_body.sunk | while | flops 2 | bytes 131189 | solution.py:102
  212.6 0.6 fusion.41
  213.2 1.4 bitcast_dynamic-update-slice_fusion.2
  214.6 0.6 fusion.41
  215.2 1.4 bitcast_dynamic-update-slice_fusion.2
  216.7 19.7 %custom-call.16 = f32[2,128,128]{1,2,0:T(8,128)S(1)} custom-call(f32[2,128,128]{2,1,0:T(8,128)S(1)} %get-tuple-element.9), custom_call_target="InvertDiagBlocksLowerTriangular" | custom-call | tf_op jit(solution)/shard_map/jit(_solve_triangular)/triangular_solve | solution.py:102
  237.6 0.6 fusion.1
  238.2 1.9 fusion.3
  240.1 1.2 pad_maximum_fusion
  241.3 2.5 reshape_reshape_reshape.4
  243.8 1.7 copy.55
  245.5 37.5 %all_to_all.39 = f32[16,32,640]{2,1,0:T(8,128)} all-to-all(f32[16,32,640]{2,1,0:T(8,128)S(1)} %bitcast.69), channel_id=1, replica_groups=mesh['row_0'=4,'row_1'=8,'row_2'=2,'col'=8] {'row_2','col'}, dimensions={0} | all-to-all | bytes 2621440 | tf_op jit(solution)/shard_map/all_to_all | solution.py:40
  283.0 1.4 reduce_sum.69
  284.5 14.5 %all_to_all.40 = f32[32,1,640]{2,1,0:T(1,128)S(1)} all-to-all(f32[32,1,640]{2,1,0:T(1,128)S(1)} %all_to_all.27), channel_id=1, replica_groups=mesh['row_0'=4,'row_1'=8,'row_2'=2,'col'=8] {'row_0','row_1'}, dimensions={0} | all-to-all | bytes 163840 | tf_op jit(solution)/shard_map/all_to_all | solution.py:47
  299.1 12.3 %all_to_all.41 = f32[32,1,640]{2,1,0:T(1,128)S(1)} all-to-all(f32[32,1,640]{2,1,0:T(1,128)S(1)} %broadcast_in_dim.79), channel_id=1, replica_groups=mesh['row_0'=4,'row_1'=8,'row_2'=2,'col'=8] {'row_0','row_1'}, dimensions={0} | all-to-all | bytes 163840 | tf_op jit(solution)/shard_map/all_to_all | solution.py:18
  311.4 1.2 broadcast_in_dim.80
  312.6 7.8 %all-to-all-start.5 = ((f32[16,32,640]{2,1,0:T(8,128)}), f32[16,32,640]{2,1,0:T(8,128)}, u32[]{:S(2)}, u32[]{:S(2)}) async-start(f32[16,32,640]{2,1,0:T(8,128)} %broadcast_in_dim.80), calls=%async_computation.5 | async-start | bytes 2621440 | tf_op jit(solution)/shard_map/all_to_all | solution.py:18
  320.4 1.0 copy.49
  321.4 31.0 %all-to-all-done.5 = f32[16,32,640]{2,1,0:T(8,128)} async-done(((f32[16,32,640]{2,1,0:T(8,128)}), f32[16,32,640]{2,1,0:T(8,128)}, u32[]{:S(2)}, u32[]{:S(2)}) %all-to-all-start.5) | async-done | bytes 1310752 | tf_op jit(solution)/shard_map/all_to_all | solution.py:18
  352.4 1.4 multiply_bitcast_fusion
  353.8 0.8 copy.48
  354.6 1.4 div.20
  (45 shorter events, 3.1 us)
Async XLA Ops:
  7.2 2.7 copy-start
  7.2 147.0 %all-gather.3.cloned.1.call-start = ((), (), s32[]{:S(2)}) async-start(), calls=%async_computation.6 | async-start | bytes 8404992 | tf_op jit(solution)/shard_map/all_gather | solution.py:91
  37.1 9.3 %copy-start.4 = (s32[256]{0:T(256)S(1)}, s32[256]{0:T(256)}, u32[]{:S(2)}) copy-start(s32[256]{0:T(256)} %param.8) | copy-start | bytes 3076
  37.1 9.4 %copy-start.1 = (bf16[512,512]{1,0:T(8,128)(2,1)S(1)}, bf16[512,512]{1,0:T(8,128)(2,1)}, u32[]{:S(2)}) copy-start(bf16[512,512]{1,0:T(8,128)(2,1)} %param.5) | copy-start | bytes 1572868
  37.1 47.4 %all-to-all-start.1 = ((bf16[16,32,3,512]{3,1,2,0:T(8,128)(2,1)}), bf16[16,32,3,512]{3,1,2,0:T(8,128)(2,1)}, u32[]{:S(2)}, u32[]{:S(2)}) async-start(bf16[16,32,3,512]{3,1,2,0:T(8,128)(2,1)} %broadcast_in_dim.75), calls=%async_computation.1 | async-start | bytes 3145728 | tf_op jit(solution)/shard_map/all_to_all | solution.py:18
  169.3 1.7 copy-start.3
  176.4 60.0 %copy-start.2 = (f32[256,512]{1,0:T(8,128)S(1)}, f32[256,512]{1,0:T(8,128)}, u32[]{:S(2)}) copy-start(f32[256,512]{1,0:T(8,128)} %convolution_subtract_fusion) | copy-start | bytes 1572868
  212.5 25.1 %copy-start.5 = (f32[512]{0:T(512)S(1)}, f32[512]{0:T(512)}, u32[]{:S(2)}) copy-start(f32[512]{0:T(512)} %param.7) | copy-start | bytes 6148
  312.6 39.8 %all-to-all-start.5 = ((f32[16,32,640]{2,1,0:T(8,128)}), f32[16,32,640]{2,1,0:T(8,128)}, u32[]{:S(2)}, u32[]{:S(2)}) async-start(f32[16,32,640]{2,1,0:T(8,128)} %broadcast_in_dim.80), calls=%async_computation.5 | async-start | bytes 2621440 | tf_op jit(solution)/shard_map/all_to_all | solution.py:18
Sparse Core Ops, SparseCore 0:
  13.0 141.0 all-gather.2
where the time goes:
time: 364 us; the launch traced here: 363 us
  waiting for transfers between devices  124 us (34%)
  blocking collectives  86.9 us (24%)
  other arithmetic  63.1 us (17%)
  local copies, waits for them, and re-layouts  45.7 us (13%)
  starting transfers between devices  17.2 us (5%)
  between operations  15.7 us (4%)
  matrix products  10.2 us (3%)
    all_to_all x2, waiting for transfers between devices, copy_for_each(): return lax.all_to_all(copies, axis, split_axis=0, concat_axis=0, tiled=True)  68.9 us
    all_gather x1, waiting for transfers between devices, body(): every_h = lax.all_gather(slot_h, ROW_COL, axis=0, tiled=True)  55.2 us
    all_to_all x1, blocking collectives, summed_on_arrival(): lax.all_to_all(parts, axis, split_axis=0, concat_axis=0, tiled=True)  37.5 us
    all_to_all x2, blocking collectives, copy_for_each(): return lax.all_to_all(copies, axis, split_axis=0, concat_axis=0, tiled=True)  34.9 us
    another operation x6, other arithmetic, body(): lower_block = jnp.linalg.cholesky(block)  34.2 us
    another operation x3, other arithmetic, body(): jax.scipy.linalg.solve_triangular(lower_block, residual.T, lower=True)  19.7 us
    all_to_all x2, starting transfers between devices, copy_for_each(): return lax.all_to_all(copies, axis, split_axis=0, concat_axis=0, tiled=True)  17.1 us
    all_to_all x1, blocking collectives, sum_by_axis(): return jnp.sum(lax.all_to_all(own, far, 0, 0, tiled=True), axis=0)  14.5 us
  transfers between devices with their start and end apart: 3, of which 3 were waited for; matrix products, arithmetic and copies ran while one was open for 5% of the time, Pallas kernels for 0%

commit v1 on v0

v1 whole, which is shorter than its diff:
```python
import functools

import jax
import jax.numpy as jnp
from jax import lax
from jax.experimental import pallas as pl
from jax.experimental.pallas import tpu as pltpu
from jax.sharding import Mesh
from jax.sharding import PartitionSpec as P

MESH = pl.DeviceIdType.MESH
AXES = ("x", "z", "c", "y")
SIZES = {"x": 4, "z": 8, "c": 2, "y": 8}
F = 512
R = 1024
B = 256
SLOTS = 4
H_SCALE = 2.0**20
HIGHEST = lax.Precision.HIGHEST


def coord(axis):
    return lax.axis_index(axis)


def peer(**offsets):
    return tuple(
        lax.rem(coord(a) + offsets[a] % SIZES[a], SIZES[a]) if a in offsets else coord(a) for a in AXES
    )


class Copies:
    def __init__(self, send_sem, recv_sem):
        self.send_sem, self.recv_sem, self.used = send_sem, recv_sem, 0

    def start(self, src, dst, device):
        copy = pltpu.make_async_remote_copy(
            src_ref=src,
            dst_ref=dst,
            send_sem=self.send_sem.at[self.used],
            recv_sem=self.recv_sem.at[self.used],
            device_id=device,
            device_id_type=MESH,
        )
        self.used += 1
        copy.start()
        return copy


def greet(peers):
    barrier = pltpu.get_barrier_semaphore()
    for device in peers:
        pl.semaphore_signal(barrier, inc=1, device_id=device, device_id_type=MESH)
    return lambda: pl.semaphore_wait(barrier, len(peers))


X_PEERS = [dict(x=d) for d in range(1, 4)]
Y_PEERS = [dict(y=d) for d in range(1, 8)]
Z_PEERS = [dict(z=d) for d in range(1, 8)]
ZC_PEERS = [dict(z=d, c=e) for d in range(8) for e in range(2) if (d, e) != (0, 0)]
CORE = dict(c=1)


def gather_kernel(sx, sh, gx, gh, ox, oh, rx, rh, tx, th, ax, ah, bx, bh, yx, yh, fx, fh, send_sem, recv_sem):
    x, z, c, y = (coord(a) for a in AXES)
    copies = Copies(send_sem, recv_sem)
    everyone = [peer(**o) for o in ZC_PEERS + X_PEERS + Y_PEERS]
    greet(everyone)()

    here = z * 2 + c
    pending = []
    for o in ZC_PEERS:
        pending.append(copies.start(sx, rx.at[here], peer(**o)))
        pending.append(copies.start(sh, rh.at[here], peer(**o)))
    rx[here] = sx[...]
    rh[here] = sh[...]
    for copy in pending:
        copy.wait()

    tx[...] = jnp.dot(
        gx[...], rx[...].reshape(16 * 16, 128), preferred_element_type=jnp.float32
    ).astype(jnp.bfloat16).reshape(4, 16, 128)
    codes = rh[...].reshape(16 * 32, 128).astype(jnp.int32)
    high = (codes + 128) >> 8
    low = codes - high * 256
    high = high.astype(jnp.float32).astype(jnp.bfloat16)
    low = low.astype(jnp.float32).astype(jnp.bfloat16)
    picked = 256.0 * jnp.dot(gh[...], high, preferred_element_type=jnp.float32) + jnp.dot(
        gh[...], low, preferred_element_type=jnp.float32
    )
    th[...] = picked.astype(jnp.int32).astype(jnp.int16).reshape(4, 2, 16, 128)

    pending = []
    for i, o in enumerate(X_PEERS):
        device = peer(**o)
        pending.append(copies.start(tx.at[device[0]], ax.at[i], device))
        pending.append(copies.start(th.at[device[0]], ah.at[i], device))
    for copy in pending:
        copy.wait()
    total_x = tx[x].astype(jnp.float32)
    total_h = th[x].astype(jnp.int32)
    for i in range(3):
        total_x = total_x + ax[i].astype(jnp.float32)
        total_h = total_h + ah[i].astype(jnp.int32)
    bx[...] = total_x.astype(jnp.bfloat16)
    bh[...] = total_h.astype(jnp.int16)

    pending = []
    for i, o in enumerate(Y_PEERS):
        pending.append(copies.start(bx, yx.at[i], peer(**o)))
        pending.append(copies.start(bh, yh.at[i], peer(**o)))
    for copy in pending:
        copy.wait()
    for i in range(7):
        total_x = total_x + yx[i].astype(jnp.float32)
        total_h = total_h + yh[i].astype(jnp.int32)
    fx[c, x, z] = total_x.astype(jnp.bfloat16)
    fh[c, x, z] = total_h.astype(jnp.int16)

    pending = []
    for o in Z_PEERS:
        pending.append(copies.start(fx.at[c, x, z], fx.at[c, x, z], peer(**o)))
        pending.append(copies.start(fh.at[c, x, z], fh.at[c, x, z], peer(**o)))
    for copy in pending:
        copy.wait()

    sibling = peer(**CORE)
    pending = []
    for o in X_PEERS:
        pending.append(copies.start(fx.at[c, x], fx.at[c, x], peer(**o)))
        pending.append(copies.start(fh.at[c, x], fh.at[c, x], peer(**o)))
    across = [
        copies.start(fx.at[c, x], fx.at[c, x], sibling),
        copies.start(fh.at[c, x], fh.at[c, x], sibling),
    ]
    for i, o in enumerate(X_PEERS):
        source = lax.rem(x + 4 - o["x"], 4)
        pending[2 * i].wait_recv()
        across.append(copies.start(fx.at[c, source], fx.at[c, source], sibling))
        pending[2 * i + 1].wait_recv()
        across.append(copies.start(fh.at[c, source], fh.at[c, source], sibling))
    for copy in pending:
        copy.wait_send()
    for copy in across:
        copy.wait()
    for core in range(2):
        for xb in range(4):
            for zb in range(8):
                rows = pl.ds((zb * 2 + core) * 16, 16)
                ox[rows, pl.ds(xb * 128, 128)] = fx[core, xb, zb]
                for j in range(2):
                    oh[rows, pl.ds((xb * 2 + j) * 128, 128)] = fh[core, xb, zb, j]


def gather_pivots(slot_x, slot_h, pick_x, pick_h):
    count = 2 * (15 + 3 + 7 + 7 + 3 + 4)
    vmem = pl.BlockSpec(memory_space=pltpu.VMEM)
    bf16, i16 = jnp.bfloat16, jnp.int16
    return pl.pallas_call(
        gather_kernel,
        out_shape=(
            jax.ShapeDtypeStruct((B, F), bf16),
            jax.ShapeDtypeStruct((B, R), i16),
        ),
        in_specs=[vmem] * 4,
        out_specs=(vmem, vmem),
        scratch_shapes=[
            pltpu.VMEM((16, 16, 128), bf16),
            pltpu.VMEM((16, 32, 128), i16),
            pltpu.VMEM((4, 16, 128), bf16),
            pltpu.VMEM((4, 2, 16, 128), i16),
            pltpu.VMEM((3, 16, 128), bf16),
            pltpu.VMEM((3, 2, 16, 128), i16),
            pltpu.VMEM((16, 128), bf16),
            pltpu.VMEM((2, 16, 128), i16),
            pltpu.VMEM((7, 16, 128), bf16),
            pltpu.VMEM((7, 2, 16, 128), i16),
            pltpu.VMEM((2, 4, 8, 16, 128), bf16),
            pltpu.VMEM((2, 4, 8, 2, 16, 128), i16),
            pltpu.SemaphoreType.DMA((count,)),
            pltpu.SemaphoreType.DMA((count,)),
        ],
        compiler_params=pltpu.CompilerParams(
            collective_id=0, has_side_effects=True, vmem_limit_bytes=32 * 2**20
        ),
    )(slot_x, slot_h, pick_x, pick_h)


CHUNKS = ((0, 3), (3, 2))


def sum_kernel(m, out, cl, a1, xl, a2, zl, a3, yl, send_sem, recv_sem):
    x, z, c, y = (coord(a) for a in AXES)
    copies = Copies(send_sem, recv_sem)
    everyone = [peer(**o) for o in [CORE] + X_PEERS + Y_PEERS + Z_PEERS]
    greet(everyone)()
    sibling = peer(**CORE)

    def core_out(o, n):
        return [copies.start(m.at[pl.ds(5 * (1 - c) + o, n)], cl.at[pl.ds(o, n)], sibling)]

    def core_in(o, n):
        a1[o : o + n] = m[pl.ds(5 * c + o, n)] + cl[o : o + n]

    def x_out(o, n):
        return [
            copies.start(a1.at[pl.ds(o, n), peer(**p)[0]], xl.at[i, pl.ds(o, n)], peer(**p))
            for i, p in enumerate(X_PEERS)
        ]

    def x_in(o, n):
        a2[o : o + n] = a1[o : o + n, x] + xl[0, o : o + n] + xl[1, o : o + n] + xl[2, o : o + n]

    def z_out(o, n):
        return [
            copies.start(a2.at[pl.ds(o, n), peer(**p)[1]], zl.at[i, pl.ds(o, n)], peer(**p))
            for i, p in enumerate(Z_PEERS)
        ]

    def z_in(o, n):
        total = a2[o : o + n, z]
        for i in range(7):
            total = total + zl[i, o : o + n]
        a3[o : o + n] = total
        yl[y, o : o + n] = total

    def y_out(o, n):
        return [copies.start(a3.at[pl.ds(o, n)], yl.at[y, pl.ds(o, n)], peer(**p)) for p in Y_PEERS]

    def y_in(o, n):
        total = yl[0, o : o + n]
        for i in range(1, 8):
            total = total + yl[i, o : o + n]
        out[pl.ds(5 * c + o, n), x, z] = total

    def back(o, n, place, peers):
        block = out.at[(pl.ds(5 * c + o, n), *place)]
        return [copies.start(block, block, peer(**p)) for p in peers]

    stages = [
        (core_out, core_in),
        (x_out, x_in),
        (z_out, z_in),
        (y_out, y_in),
        (lambda o, n: back(o, n, (x, z), Z_PEERS), None),
        (lambda o, n: back(o, n, (x,), X_PEERS), None),
        (lambda o, n: back(o, n, (), [CORE]), None),
    ]
    flying = {chunk: stages[0][0](*chunk) for chunk in CHUNKS}
    for s in range(len(stages)):
        for chunk in CHUNKS:
            for copy in flying[chunk]:
                copy.wait()
            if stages[s][1] is not None:
                stages[s][1](*chunk)
            if s + 1 < len(stages):
                flying[chunk] = stages[s + 1][0](*chunk)


def sum_everywhere(m):
    count = len(CHUNKS) * (1 + 3 + 7 + 7 + 7 + 3 + 1)
    vmem = pl.BlockSpec(memory_space=pltpu.VMEM)
    f32 = jnp.float32
    return pl.pallas_call(
        sum_kernel,
        out_shape=jax.ShapeDtypeStruct((10, 4, 8, 8, 128), f32),
        in_specs=[vmem],
        out_specs=vmem,
        scratch_shapes=[
            pltpu.VMEM((5, 4, 8, 8, 128), f32),
            pltpu.VMEM((5, 4, 8, 8, 128), f32),
            pltpu.VMEM((3, 5, 8, 8, 128), f32),
            pltpu.VMEM((5, 8, 8, 128), f32),
            pltpu.VMEM((7, 5, 8, 128), f32),
            pltpu.VMEM((5, 8, 128), f32),
            pltpu.VMEM((8, 5, 8, 128), f32),
            pltpu.SemaphoreType.DMA((count,)),
            pltpu.SemaphoreType.DMA((count,)),
        ],
        compiler_params=pltpu.CompilerParams(
            collective_id=1, has_side_effects=True, vmem_limit_bytes=32 * 2**20
        ),
    )(m)


def kernel_of(left, right):
    cross_term = jnp.dot(left, right.T, preferred_element_type=jnp.float32)
    left_norms = jnp.sum(jnp.square(left.astype(jnp.float32)), axis=1)
    right_norms = jnp.sum(jnp.square(right.astype(jnp.float32)), axis=1)
    distance = left_norms[:, None] + right_norms[None, :] - 2.0 * cross_term
    quarter = jnp.exp(-(0.25 / F) * distance)
    half = quarter * quarter
    return 0.5 * quarter + 0.3 * half + 0.2 * (half * half)


def body(features, factor, ip_weights, pivot_owner, pivot_position):
    x, z, c, y = (coord(a) for a in AXES)
    me = ((x * 8 + z) * 2 + c) * 8 + y
    same_owner = pivot_owner[:, None] == pivot_owner[None, :]
    earlier = jnp.arange(B)[None, :] < jnp.arange(B)[:, None]
    rank = jnp.sum((same_owner & earlier).astype(jnp.int32), axis=1)
    chosen = (pivot_owner == me)[None, :] & (rank[None, :] == jnp.arange(SLOTS)[:, None])
    rows = jnp.sum(jnp.where(chosen, pivot_position[None, :], 0), axis=1)
    slot_x = features[rows].reshape(16, 128)
    slot_h = jnp.round(factor[rows] * H_SCALE).astype(jnp.int16).reshape(32, 128)

    first = (z * 2 + c) * 16
    owner = lax.dynamic_slice(pivot_owner, (first,), (16,))
    order = lax.dynamic_slice(rank, (first,), (16,))
    near = (owner // 128 == x) & (owner % 8 == y)
    line = (owner // 8) % 16
    row_x = jnp.where(near, line * 16 + order * 4, -64)
    row_h = jnp.where(near, line * 32 + order * 8, -64)
    pick_x = (
        (row_x[None, :] + jnp.arange(4)[:, None]).reshape(64, 1) == jnp.arange(256)[None, :]
    ).astype(jnp.bfloat16)
    pick_h = (
        (row_h[None, :] + jnp.arange(8)[:, None]).reshape(128, 1) == jnp.arange(512)[None, :]
    ).astype(jnp.bfloat16)
    pivot_x, pivot_h = gather_pivots(slot_x, slot_h, pick_x, pick_h)
    pivot_h = pivot_h.astype(jnp.float32) * (1.0 / H_SCALE)

    residual = kernel_of(features, pivot_x) - jnp.dot(factor, pivot_h.T, precision=HIGHEST)
    block = kernel_of(pivot_x, pivot_x) - jnp.dot(pivot_h, pivot_h.T, precision=HIGHEST)
    weighted = residual * ip_weights[:, None]
    local = jnp.dot(
        weighted.T, jnp.concatenate([factor, residual], axis=1), precision=HIGHEST
    )
    total = sum_everywhere(local.reshape(B, 10, 128).swapaxes(0, 1).reshape(10, 4, 8, 8, 128))
    total = total.reshape(10, B, 128).swapaxes(0, 1).reshape(B, 1280)

    lower = jnp.linalg.cholesky(block)
    inverse = jax.scipy.linalg.solve_triangular(lower, jnp.eye(B, dtype=jnp.float32), lower=True)
    new_columns = jnp.dot(residual, inverse.T, precision=HIGHEST)
    gram = jnp.dot(inverse, total, precision=HIGHEST)
    right = jnp.dot(gram[:, R:], inverse.T, precision=HIGHEST)
    gram = jnp.concatenate([gram[:, :R], right], axis=1)
    return (new_columns, gram / (512 * 512))


def solution(mesh):
    torus = Mesh(mesh.devices.reshape(4, 8, 2, 8), AXES)
    spread = P(AXES)
    in_specs = (P(AXES, None), P(AXES, None), spread, P(), P())
    out_specs = (P(AXES, None), P())
    return jax.shard_map(body, mesh=torus, in_specs=in_specs, out_specs=out_specs, check_vma=False)
```

time: 364 us -> 180 us (0.49)
  waiting for transfers between devices: 124 us -> 0 us
  blocking collectives: 86.9 us -> 0 us
  Pallas kernels: 0 us -> 84.5 us
  local copies, waits for them, and re-layouts: 45.7 us -> 12.9 us
  starting transfers between devices: 17.2 us -> 0 us
  between operations: 15.7 us -> 2.24 us
  matrix products: 10.2 us -> 17.5 us
    all_to_all x4 -> x0, blocking collectives: 86.9 us -> none  [the longest x1 37.5 us: summed_on_arrival(): lax.all_to_all(parts, axis, split_axis=0, concat_axis=0, tiled=True)]
    pallas_call x0 -> x2, Pallas kernels: none -> 84.5 us  [the longest x1 45.3 us: gather_pivots(): pl.pallas_call(gather_kernel, out_shape=(jax.ShapeDtypeStruct((B, F), bf1...]
    all_to_all x2 -> x0, waiting for transfers between devices: 68.9 us -> none  [copy_for_each(): return lax.all_to_all(copies, axis, split_axis=0, concat_axis=0, tiled=True)]
    all_gather x1 -> x0, waiting for transfers between devices: 55.2 us -> none  [body(): every_h = lax.all_gather(slot_h, ROW_COL, axis=0, tiled=True)]
    all_to_all x2 -> x0, starting transfers between devices: 17.1 us -> none  [copy_for_each(): return lax.all_to_all(copies, axis, split_axis=0, concat_axis=0, tiled=True)]
    unnamed x15 -> x8, local copies, waits for them, and re-layouts: 11.8 us -> 0.02 us
    another operation x12 -> x9, local copies, waits for them, and re-layouts: 13.4 us -> 5.3 us  [the longest x1 5.06 us: in_order(): return jnp.moveaxis(parts, 0, dim).reshape(dims)]
    gather x4 -> x2, local copies, waits for them, and re-layouts: 9.41 us -> 3.84 us  [the longest x1 2.16 us: body(): factor[rows] * H_SCALE]
  transfers between devices with their start and end apart: 3 -> 0, of which waited for: 3 -> 0; matrix products, arithmetic and copies ran while one was open for 5% -> 0% of each run, Pallas kernels for 0% -> 0%
where the time goes in v1:
time: 180 us; the launch traced here: 179 us
  Pallas kernels  84.5 us (47%)
  other arithmetic  61.9 us (34%)
  matrix products  17.5 us (10%)
  local copies, waits for them, and re-layouts  12.9 us (7%)
  between operations  2.24 us (1%)
    pallas_call x1, Pallas kernels, gather_pivots(): pl.pallas_call(gather_kernel, out_shape=(jax.ShapeDtypeStruct((B, F), bf1...  45.3 us
    pallas_call x1, Pallas kernels, sum_everywhere(): pl.pallas_call(sum_kernel, out_shape=jax.ShapeDtypeStruct((10, 4, 8, 8, 1...  39.2 us
    another operation x6, other arithmetic, body(): lower = jnp.linalg.cholesky(block)  34.1 us
    another operation x3, other arithmetic, body(): jax.scipy.linalg.solve_triangular(lower, jnp.eye(B, dtype=jnp.float32), l...  20.5 us
    dot_general x1, matrix products, body(): jnp.dot(weighted.T, jnp.concatenate([factor, residual], axis=1), precisio...  5.31 us
    another operation x6, local copies, waits for them, and re-layouts  5.2 us

profile of v1, /device:TPU:1, one launch (start us, length us, event | category | flops | bytes accessed | tf_op | source)
XLA Modules:
  0.0 179.1 jit_solution(1449287886846882132)
XLA Ops:
  0.6 0.7 broadcast_compare_fusion
  1.3 0.1 triangular_solve.63
  1.4 0.9 convert_reduce_fusion
  2.3 0.8 select_reduce_fusion.2
  3.1 0.8 add_select_fusion
  3.9 0.1 add_select_fusion.1
  4.0 0.1 add.166
  4.1 1.2 multiply_reduce_fusion
  5.3 0.1 add.171
  5.4 1.7 gather_fusion
  7.1 2.2 %gather_fusion.1 = f32[4,1024]{1,0:T(4,128)S(1)} fusion(f32[512,1024]{1,0:T(8,128)} %param.6, s32[1024]{0:T(1024)S(1)} %pad_clamp_fusion), kind=kCustom, calls=%fused_computation.1 | custom fusion | bytes 32784 | tf_op jit(solution)/shard_map/gather | solution.py:305
  9.3 0.1 fusion.32.gx
  9.4 0.1 fusion.21.gh
  9.5 45.3 %shard_map.68 = (bf16[256,512]{1,0:T(8,128)(2,1)S(1)}, s16[256,1024]{1,0:T(8,128)(2,1)S(1)}) custom-call(bf16[16,128]{1,0:T(8,128)(2,1)S(1)} %reshape.98.sx, s16[32,128]{1,0:T(8,128)(2,1)S(1)} %convert_element_type.31.sh, bf16[64,256]{1,0:T(8,128)(2,1)S(1)} %fusion.32.gx, bf16[128,512]{1,0:T(8,128)(2,1)S(1)} %fusion.21.gh), custom_call_target="tpu_custom_call" | custom-call | tf_op jit(solution)/shard_map/pallas_call | solution.py:159
  54.8 0.1 multiply_reduce_fusion.1
  55.0 1.3 fusion.9
  56.3 0.8 copy.26
  57.2 1.4 fusion.8
  58.6 2.1 %fusion.4 = f32[512,256]{0,1:T(8,128)S(1)} fusion(f32[512,1024]{1,0:T(8,128)S(1)} %copy-done, s16[256,1024]{1,0:T(8,128)(2,1)S(1)} %get-tuple-element.5, f32[512,256]{0,1:T(8,128)S(1)} %fusion.8), kind=kOutput, calls=%fused_computation.10 | convolution fusion | flops 1612185600 | bytes 3670016 | tf_op jit(solution)/shard_map/dot_general | solution.py:323
  60.7 1.0 fusion.26
  61.6 0.1 copy.24
  61.8 0.1 copy.25
  61.9 1.3 fusion.16
  63.3 11.7 %cholesky.50 = f32[128,128]{1,0:T(8,128)S(1)} custom-call(f32[128,128]{1,0:T(8,128)S(1)} %cholesky.118), custom_call_target="Cholesky" | custom-call | tf_op jit(solution)/shard_map/jit(cholesky)/cholesky | solution.py:332
  75.0 9.9 %custom-call.15 = f32[1,128,128]{1,2,0:T(8,128)S(1)} custom-call(f32[1,128,128]{2,1,0:T(8,128)S(1)} %get-tuple-element.30), custom_call_target="InvertDiagBlocksLowerTriangular" | custom-call | tf_op jit(solution)/shard_map/jit(cholesky)/cholesky | solution.py:332
  85.0 1.0 constant_dynamic-update-slice_fusion.1
  86.1 1.1 convolution_subtract_fusion.1
  87.2 11.7 %cholesky.105 = f32[128,128]{1,0:T(8,128)S(1)} custom-call(f32[128,128]{1,0:T(8,128)S(1)} %convolution_subtract_fusion.1), custom_call_target="Cholesky" | custom-call | tf_op jit(solution)/shard_map/jit(cholesky)/cholesky | solution.py:332
  98.9 0.6 compare_reduce_fusion
  100.9 5.2 %while.1 = (s32[]{:T(128)}, f32[256,256]{1,0:T(8,128)S(1)}, s32[2,2]{1,0:T(2,128)S(1)}, f32[2,128,128]{2,1,0:T(8,128)}, s32[]{:T(128)}) while((s32[]{:T(128)}, f32[256,256]{1,0:T(8,128)S(1)}, s32[2,2]{1,0:T(2,128)S(1)}, f32[2,128,128]{2,1,0:T(8,128)}, s32[]{:T(128)}) %tuple.31), condition=%wide.while_cond, body=%wide.while_body.sunk | while | flops 2 | bytes 132205 | solution.py:333
  100.9 0.6 fusion.55
  101.5 2.0 %bitcast_dynamic-update-slice_fusion.2 = f32[2,128,128]{2,1,0:T(8,128)} fusion(f32[2,128,128]{2,1,0:T(8,128)} %get-tuple-element.75, s32[]{:T(128)S(6)} %copy.40, f32[256,256]{1,0:T(8,128)S(1)} %get-tuple-element.78, s32[]{:T(128)} %bitcast.70, s32[]{:T(128)} %bitcast.71), kind=kLoop, calls=%fused_computation.2.clone.1 | loop fusion | bytes 132100 | tf_op jit(solution)/shard_map/jit(_solve_triangular)/triangular_solve
  103.5 0.6 fusion.55
  104.1 2.0 %bitcast_dynamic-update-slice_fusion.2 = f32[2,128,128]{2,1,0:T(8,128)} fusion(f32[2,128,128]{2,1,0:T(8,128)} %get-tuple-element.75, s32[]{:T(128)S(6)} %copy.40, f32[256,256]{1,0:T(8,128)S(1)} %get-tuple-element.78, s32[]{:T(128)} %bitcast.70, s32[]{:T(128)} %bitcast.71), kind=kLoop, calls=%fused_computation.2.clone.1 | loop fusion | bytes 132100 | tf_op jit(solution)/shard_map/jit(_solve_triangular)/triangular_solve
  106.1 20.5 %custom-call.16 = f32[2,128,128]{1,2,0:T(8,128)S(1)} custom-call(f32[2,128,128]{2,1,0:T(8,128)} %get-tuple-element.13), custom_call_target="InvertDiagBlocksLowerTriangular" | custom-call | tf_op jit(solution)/shard_map/jit(_solve_triangular)/triangular_solve | solution.py:333
  126.6 0.3 fusion.24
  126.9 0.3 convolution_subtract_fusion
  127.2 0.3 fusion.28
  127.5 1.8 %fusion.23 = f32[512,256]{1,0:T(8,128)} fusion(f32[512,256]{0,1:T(8,128)S(1)} %fusion.4, f32[128,256]{1,0:T(8,128)S(1)} %fusion.28, f32[128,256]{1,0:T(8,128)S(1)} %fusion.24), kind=kOutput, calls=%fused_computation.45 | convolution fusion | flops 402718720 | bytes 1310720 | tf_op jit(solution)/shard_map/dot_general | solution.py:334
  129.3 0.2 copy.27
  129.5 5.3 %fusion = f32[256,1280]{0,1:T(8,128)} fusion(f32[512,256]{1,0:T(8,128)S(1)} %copy.27, f32[512,1024]{1,0:T(8,128)S(1)} %copy-done, f32[512,256]{0,1:T(8,128)S(1)} %fusion.4, f32[512]{0:T(512)S(1)} %copy-done.3), kind=kOutput, calls=%fused_computation.4 | convolution fusion | flops 2014052352 | bytes 4458496 | tf_op jit(solution)/shard_map/dot_general | solution.py:326
  134.8 1.7 copy.29
  136.5 39.2 %shard_map.69 = f32[10,4,8,8,128]{4,3,2,1,0:T(8,128)S(1)} custom-call(f32[10,4,8,8,128]{4,3,2,1,0:T(8,128)S(1)} %bitcast.72), custom_call_target="tpu_custom_call" | custom-call | tf_op jit(solution)/shard_map/pallas_call | solution.py:264
  175.7 0.4 copy.30
  176.1 1.3 fusion.22
  177.4 0.4 fusion.13
  177.8 0.1 slice.71
  177.9 1.2 maximum_multiply_fusion
  (25 shorter events, 0.3 us)
Async XLA Ops:
  55.0 3.6 %copy-start = (f32[512,1024]{1,0:T(8,128)S(1)}, f32[512,1024]{1,0:T(8,128)}, u32[]{:S(2)}) copy-start(f32[512,1024]{1,0:T(8,128)} %param.6) | copy-start | bytes 6291460
  56.3 0.8 copy-start.1
  63.2 11.8 %copy-start.2 = (f32[256,256]{1,0:T(8,128)}, f32[256,256]{1,0:T(8,128)S(1)}, u32[]{:S(2)}) copy-start(f32[256,256]{1,0:T(8,128)S(1)} %fusion.16) | copy-start | bytes 786436
  127.2 2.3 %copy-start.3 = (f32[512]{0:T(512)S(1)}, f32[512]{0:T(512)}, u32[]{:S(2)}) copy-start(f32[512]{0:T(512)} %param.7) | copy-start | bytes 6148

commit v2 on v1

v2 whole, which is shorter than its diff:
```python
import jax
import jax.numpy as jnp
from jax import lax
from jax.experimental import pallas as pl
from jax.experimental.pallas import tpu as pltpu
from jax.sharding import Mesh
from jax.sharding import PartitionSpec as P

MESH = pl.DeviceIdType.MESH
AXES = ("x", "z", "c", "y")
SIZES = {"x": 4, "z": 8, "c": 2, "y": 8}
F = 512
R = 1024
B = 256
H_SCALE = 2.0**20


def coord(axis):
    return lax.axis_index(axis)


def peer(**offsets):
    return tuple(
        lax.rem(coord(a) + offsets[a] % SIZES[a], SIZES[a]) if a in offsets else coord(a) for a in AXES
    )


class Copies:
    def __init__(self, send_sem, recv_sem):
        self.send_sem, self.recv_sem, self.used = send_sem, recv_sem, 0

    def start(self, src, dst, device):
        copy = pltpu.make_async_remote_copy(
            src_ref=src,
            dst_ref=dst,
            send_sem=self.send_sem.at[self.used],
            recv_sem=self.recv_sem.at[self.used],
            device_id=device,
            device_id_type=MESH,
        )
        self.used += 1
        copy.start()
        return copy


def greet(peers):
    barrier = pltpu.get_barrier_semaphore()
    for device in peers:
        pl.semaphore_signal(barrier, inc=1, device_id=device, device_id_type=MESH)
    return lambda: pl.semaphore_wait(barrier, len(peers))


X_PEERS = [dict(x=d) for d in (1, 3, 2)]
Y_PEERS = [dict(y=d) for d in range(1, 8)]
Z_STEPS = (0, 1, 7, 2, 6, 3, 5, 4)
Z_PEERS = [dict(z=d) for d in Z_STEPS[1:]]
ZC_PEERS = [dict(z=d, c=e) for d in Z_STEPS for e in range(2) if (d, e) != (0, 0)]
CORE = dict(c=1)
Z_GROUPS = ((0, 5), (5, 3))


CHUNKS = ((0, 3), (3, 2))
W = 16


def split(values, count):
    out = []
    for _ in range(count - 1):
        part = values.astype(jnp.bfloat16)
        out.append(part)
        values = values - part.astype(jnp.float32)
    return out + [values.astype(jnp.bfloat16)]


def product(left, right, dims, count):
    order = {2: ((0, 0), (0, 1), (1, 0)), 3: ((0, 0), (0, 1), (1, 0), (0, 2), (2, 0), (1, 1))}[count]
    lhs = jnp.concatenate([left[i] for i, _ in order], axis=dims[0])
    rhs = jnp.concatenate([right[j] for _, j in order], axis=dims[1])
    return lax.dot_general(
        lhs, rhs, (((dims[0],), (dims[1],)), ((), ())), preferred_element_type=jnp.float32
    )


def row_norms(samples):
    ones = jnp.ones((8, F), jnp.bfloat16)
    norms = sum(
        lax.dot_general(ones, s, (((1,), (1,)), ((), ())), preferred_element_type=jnp.float32)
        for s in split(jnp.square(samples.astype(jnp.float32)), 2)
    )
    return norms[0:1]


def transposed_kernel(pivots, samples, norms):
    cross = lax.dot_general(
        pivots, samples, (((1,), (1,)), ((), ())), preferred_element_type=jnp.float32
    )
    pivot_norms = jnp.sum(jnp.square(pivots.astype(jnp.float32)), axis=1, keepdims=True)
    distance = pivot_norms + norms - 2.0 * cross
    quarter = jnp.exp(-(0.25 / F) * distance)
    half = quarter * quarter
    return 0.5 * quarter + 0.3 * half + 0.2 * (half * half)


def pivot_panel(p, base, a, xi):
    first = pl.multiple_of(p * W, W)
    rows = pl.ds(first, W)
    lanes = B - base
    s = a[rows, base:]
    xs = xi[rows, :]
    sub = lax.broadcasted_iota(jnp.int32, (W, 1), 0)
    lane = lax.broadcasted_iota(jnp.int32, (W, lanes), 1) + base
    columns = [
        jnp.sum(jnp.where(lane == first + j, s, 0.0), axis=1, keepdims=True) for j in range(W)
    ]
    pivots = jnp.ones((W, 1), jnp.float32)
    for j in range(W):
        pivot = columns[j][j : j + 1]
        factor = jnp.where(sub > j, columns[j] * (1.0 / pivot), 0.0)
        for k in range(j + 1, W):
            columns[k] = columns[k] - factor * columns[k][j : j + 1]
        s = s - factor * s[j : j + 1]
        xs = xs - factor * xs[j : j + 1]
        pivots = jnp.where(sub == j, pivot, pivots)
    scale = lax.rsqrt(pivots)
    xs = xs * scale
    later = jnp.where(lane >= first + W, s * scale, 0.0)
    update = product(
        split(later, 3), split(jnp.concatenate([later, xs], axis=1), 3), (0, 0), 3
    )
    a[base:, base:] = a[base:, base:] - update[:, :lanes]
    xi[base:, :] = xi[base:, :] - update[:, lanes:]
    xi[rows, :] = xs


def eliminate(first, last, a, xi):
    base = 0 if last * W <= B // 2 else B // 2

    def step(p, carry):
        pivot_panel(p, base, a, xi)
        return carry

    lax.fori_loop(first, last, step, 0)


def code_parts(codes):
    codes = codes.astype(jnp.int32)
    high = (codes + 128) >> 8
    return high.astype(jnp.float32), (codes - high * 256).astype(jnp.float32)


def whole_kernel(
    owner_hbm, position_hbm, weights_hbm, features_hbm, factor_hbm, columns_out, gram_out,
    owner, position, weights, features, factor, factor_hi, factor_lo, norms, table,
    sx, sh, rx, rh, tx, th, ax, ah, bx, bh, yx, yh, fx, fh,
    px, pa, pb, rt, m, a, xi, f, cl, a1, xl, a2, zl, a3, yl,
    load_sem, send_sem, recv_sem,
):
    x, z, c, y = (coord(axis) for axis in AXES)
    copies = Copies(send_sem, recv_sem)
    small = [
        pltpu.make_async_copy(source, target, load_sem.at[5 + i])
        for i, (source, target) in enumerate(
            ((owner_hbm, owner), (position_hbm, position), (weights_hbm, weights))
        )
    ]
    for load in small:
        load.start()
    load_x = pltpu.make_async_copy(features_hbm, features, load_sem.at[0])
    load_x.start()
    loads = []
    for i in range(4):
        rows = pl.ds(i * 128, 128)
        loads.append(
            pltpu.make_async_copy(factor_hbm.at[rows], factor.at[rows], load_sem.at[1 + i])
        )
        loads[i].start()
    wait_for_all = greet([peer(**o) for o in ZC_PEERS + X_PEERS + Y_PEERS])
    sibling = peer(**CORE)

    me = ((x * 8 + z) * 2 + c) * 8 + y
    for load in small:
        load.wait()
    row_owner = owner[...]
    col_owner = jnp.broadcast_to(row_owner.astype(jnp.float32), (B, B)).T.astype(jnp.int32)
    i_row = lax.broadcasted_iota(jnp.int32, (B, B), 0)
    i_col = lax.broadcasted_iota(jnp.int32, (B, B), 1)
    same = col_owner == row_owner
    row_rank = jnp.sum(jnp.where(same & (i_row < i_col), 1.0, 0.0), axis=0, keepdims=True)
    col_rank = jnp.sum(jnp.where(same & (i_col < i_row), 1.0, 0.0), axis=1, keepdims=True)
    near = (col_owner[:, :128] // 128 == x) & (col_owner[:, :128] % 8 == y)
    place = (col_owner[:, :128] // 8) % 16 * 4 + col_rank.astype(jnp.int32)
    table[...] = jnp.where(near, place, -64)

    slot = lax.broadcasted_iota(jnp.int32, (48, B), 0)
    slot = jnp.where(slot < 16, slot // 4, (slot - 16) // 8)
    mine = (row_owner == me) & (row_rank.astype(jnp.int32) == slot)
    at = jnp.sum(
        jnp.where(mine, position[...].astype(jnp.float32) + 1.0, 0.0), axis=1, keepdims=True
    ).astype(jnp.int32) - 1
    pick = jnp.where(lax.broadcasted_iota(jnp.int32, (48, 512), 1) == at, 1.0, 0.0).astype(jnp.bfloat16)
    load_x.wait()
    rows_x = jnp.dot(pick[:16], features[...], preferred_element_type=jnp.float32)
    block_x = lax.broadcasted_iota(jnp.int32, (16, 128), 0) % 4
    sx[...] = sum(
        jnp.where(block_x == b, rows_x[:, b * 128 : b * 128 + 128], 0.0) for b in range(4)
    ).astype(jnp.bfloat16)
    for load in loads:
        load.wait()

    def cut(i, carry):
        rows = pl.ds(pl.multiple_of(i * 64, 64), 64)
        factor_hi[rows, :], factor_lo[rows, :] = split(factor[rows, :], 2)
        return carry

    lax.fori_loop(0, 8, cut, 0)
    rows_h = jnp.dot(pick[16:], factor_hi[...], preferred_element_type=jnp.float32) + jnp.dot(
        pick[16:], factor_lo[...], preferred_element_type=jnp.float32
    )
    block_h = lax.broadcasted_iota(jnp.int32, (32, 128), 0) % 8
    own_h = sum(jnp.where(block_h == b, rows_h[:, b * 128 : b * 128 + 128], 0.0) for b in range(8))
    sh[...] = jnp.round(own_h * H_SCALE).astype(jnp.int32).astype(jnp.int16)

    wait_for_all()
    here = z * 2 + c
    pending = []
    for o in ZC_PEERS:
        pending.append(copies.start(sx, rx.at[here], peer(**o)))
        pending.append(copies.start(sh, rh.at[here], peer(**o)))
    rx[here] = sx[...]
    rh[here] = sh[...]
    norms[...] = row_norms(features[...])
    target = table[pl.ds(pl.multiple_of(here * 16, 16), 16), :][:, :1]
    target_x = jnp.concatenate([target * 4 + b for b in range(4)], axis=0)
    target_h = jnp.concatenate([target * 8 + b for b in range(8)], axis=0)
    pick_x = jnp.where(
        lax.broadcasted_iota(jnp.int32, (64, 256), 1) == target_x, 1.0, 0.0
    ).astype(jnp.bfloat16)
    pick_h = jnp.where(
        lax.broadcasted_iota(jnp.int32, (128, 512), 1) == target_h, 1.0, 0.0
    ).astype(jnp.bfloat16)
    for copy in pending:
        copy.wait()
    tx[...] = jnp.dot(
        pick_x, rx[...].reshape(16 * 16, 128), preferred_element_type=jnp.float32
    ).astype(jnp.bfloat16).reshape(4, 16, 128)
    high, low = code_parts(rh[...].reshape(16 * 32, 128))
    picked = 256.0 * jnp.dot(
        pick_h, high.astype(jnp.bfloat16), preferred_element_type=jnp.float32
    ) + jnp.dot(pick_h, low.astype(jnp.bfloat16), preferred_element_type=jnp.float32)
    th[...] = picked.astype(jnp.int32).astype(jnp.int16).reshape(4, 2, 16, 128)

    pending = []
    for i, o in enumerate(X_PEERS):
        device = peer(**o)
        pending.append(copies.start(tx.at[device[0]], ax.at[i], device))
        pending.append(copies.start(th.at[device[0]], ah.at[i], device))
    for copy in pending:
        copy.wait()
    total_x = tx[x].astype(jnp.float32)
    total_h = th[x].astype(jnp.int32)
    for i in range(3):
        total_x = total_x + ax[i].astype(jnp.float32)
        total_h = total_h + ah[i].astype(jnp.int32)
    bx[...] = total_x.astype(jnp.bfloat16)
    bh[...] = total_h.astype(jnp.int16)

    pending = []
    for i, o in enumerate(Y_PEERS):
        pending.append(copies.start(bx, yx.at[i], peer(**o)))
        pending.append(copies.start(bh, yh.at[i], peer(**o)))
    for copy in pending:
        copy.wait()
    for i in range(7):
        total_x = total_x + yx[i].astype(jnp.float32)
        total_h = total_h + yh[i].astype(jnp.int32)
    fx[c, x, 0] = total_x.astype(jnp.bfloat16)
    fh[c, x, 0] = total_h.astype(jnp.int16)

    along_z = []
    for i, o in enumerate(Z_PEERS):
        along_z.append(copies.start(fx.at[c, x, 0], fx.at[c, x, i + 1], peer(**o)))
        along_z.append(copies.start(fh.at[c, x, 0], fh.at[c, x, i + 1], peer(**o)))
    along_x, across = [], []
    for first, size in Z_GROUPS:
        for i in range(max(first, 1), first + size):
            along_z[2 * i - 2].wait_recv()
            along_z[2 * i - 1].wait_recv()
        part_x, part_h = (ref.at[c, x, pl.ds(first, size)] for ref in (fx, fh))
        for o in X_PEERS:
            along_x.append(copies.start(part_x, part_x, peer(**o)))
            along_x.append(copies.start(part_h, part_h, peer(**o)))
        across.append(copies.start(part_x, part_x, sibling))
        across.append(copies.start(part_h, part_h, sibling))
    for g, (first, size) in enumerate(Z_GROUPS):
        for i, o in enumerate(X_PEERS):
            source = lax.rem(x + 4 - o["x"], 4)
            for j, ref in enumerate((fx, fh)):
                part = ref.at[c, source, pl.ds(first, size)]
                along_x[(g * 3 + i) * 2 + j].wait_recv()
                across.append(copies.start(part, part, sibling))

    def unpack(core):
        def step(i, carry):
            odd = i % 2
            back = odd * ((i + 1) // 2) + (1 - odd) * (8 - i // 2)
            rows = pl.ds(pl.multiple_of((((z + 8 - back) % 8) * 2 + core) * 16, 16), 16)
            for xb in range(4):
                px[rows, xb * 128 : xb * 128 + 128] = fx[core, xb, i]
                for j in range(2):
                    high, low = code_parts(fh[core, xb, i, j])
                    at = (xb * 2 + j) * 128
                    pa[rows, at : at + 128] = (high * (256.0 / H_SCALE)).astype(jnp.bfloat16)
                    pb[rows, at : at + 128] = (low * (1.0 / H_SCALE)).astype(jnp.bfloat16)
            return carry

        lax.fori_loop(0, 8, step, 0)

    unpack(c)
    for copy in along_z + along_x:
        copy.wait_send()
    for copy in across:
        copy.wait()
    unpack(1 - c)

    def local(i, carry):
        span = pl.ds(pl.multiple_of(i * 256, 256), 256)
        h = [factor_hi[span, :], factor_lo[span, :]]
        residual = transposed_kernel(px[...], features[span, :], norms[:, span]) - product(
            [pa[...], pb[...]], h, (1, 1), 2
        )
        rt[i] = residual
        weighted = split(residual * weights[i], 2)
        left = product(weighted, h, (1, 0), 2)
        right = product(weighted, split(residual, 2), (1, 1), 2)
        both = jnp.concatenate([left, right], axis=1)
        for k in range(10):
            m[k] = m[k] + both[:, k * 128 : k * 128 + 128].reshape(4, 8, 8, 128)
        return carry

    m[...] = jnp.zeros_like(m)
    lax.fori_loop(0, 2, local, 0)

    def core_out(o, n):
        return [copies.start(m.at[pl.ds(5 * (1 - c) + o, n)], cl.at[pl.ds(o, n)], sibling)]

    def core_in(o, n):
        a1[o : o + n] = m[pl.ds(5 * c + o, n)] + cl[o : o + n]

    def x_out(o, n):
        return [
            copies.start(a1.at[pl.ds(o, n), peer(**p)[0]], xl.at[i, pl.ds(o, n)], peer(**p))
            for i, p in enumerate(X_PEERS)
        ]

    def x_in(o, n):
        a2[o : o + n] = a1[o : o + n, x] + xl[0, o : o + n] + xl[1, o : o + n] + xl[2, o : o + n]

    def z_out(o, n):
        return [
            copies.start(a2.at[pl.ds(o, n), peer(**p)[1]], zl.at[i, pl.ds(o, n)], peer(**p))
            for i, p in enumerate(Z_PEERS)
        ]

    def z_in(o, n):
        total = a2[o : o + n, z]
        for i in range(7):
            total = total + zl[i, o : o + n]
        a3[o : o + n] = total
        yl[y, o : o + n] = total

    def y_out(o, n):
        return [copies.start(a3.at[pl.ds(o, n)], yl.at[y, pl.ds(o, n)], peer(**p)) for p in Y_PEERS]

    def y_in(o, n):
        total = yl[0, o : o + n]
        for i in range(1, 8):
            total = total + yl[i, o : o + n]
        f[pl.ds(5 * c + o, n), x, z] = total

    def back(o, n, place, peers):
        block = f.at[(pl.ds(5 * c + o, n), *place)]
        return [copies.start(block, block, peer(**p)) for p in peers]

    def begin_block():
        h = [pa[...], pb[...]]
        a[...] = transposed_kernel(px[...], px[...], row_norms(px[...])) - product(h, h, (1, 1), 2)
        row = lax.broadcasted_iota(jnp.int32, (B, B), 0)
        column = lax.broadcasted_iota(jnp.int32, (B, B), 1)
        xi[...] = jnp.where(row == column, 1.0, 0.0)

    def columns_of(i):
        flipped = product(split(xi[...], 3), split(rt[i], 3), (1, 0), 3)
        columns_out[i * 256 : (i + 1) * 256, :] = flipped.T

    beside = [
        [begin_block, lambda: eliminate(0, 2, a, xi)],
        [lambda: eliminate(2, 8, a, xi)],
        [lambda: eliminate(8, 12, a, xi)],
        [lambda: eliminate(12, 16, a, xi)],
        [lambda: columns_of(0)],
        [lambda: columns_of(1)],
        [],
    ]
    stages = [
        (core_out, core_in),
        (x_out, x_in),
        (z_out, z_in),
        (y_out, y_in),
        (lambda o, n: back(o, n, (x, z), Z_PEERS), None),
        (lambda o, n: back(o, n, (x,), X_PEERS), None),
        (lambda o, n: back(o, n, (), [CORE]), None),
    ]
    flying = {chunk: stages[0][0](*chunk) for chunk in CHUNKS}
    for s in range(len(stages)):
        for work in beside[s]:
            work()
        for chunk in CHUNKS:
            for copy in flying[chunk]:
                copy.wait()
            if stages[s][1] is not None:
                stages[s][1](*chunk)
            if s + 1 < len(stages):
                flying[chunk] = stages[s + 1][0](*chunk)

    inverse = split(xi[...], 3)
    scaled = 1.0 / (512 * 512)

    def total_of(k):
        return jnp.concatenate([f[k].reshape(B, 128), f[k + 1].reshape(B, 128)], axis=1)

    for k in range(0, 8, 2):
        gram_out[:, k * 128 : k * 128 + 256] = scaled * product(inverse, split(total_of(k), 3), (1, 0), 3)
    right = product(inverse, split(total_of(8), 3), (1, 0), 3)
    gram_out[:, R:] = scaled * product(split(right, 3), inverse, (1, 1), 3)


def run(features, factor, ip_weights, pivot_owner, pivot_position):
    count = 92 + len(CHUNKS) * 29
    vmem = pl.BlockSpec(memory_space=pltpu.VMEM)
    hbm = pl.BlockSpec(memory_space=pltpu.HBM)
    f32, bf16, i16 = jnp.float32, jnp.bfloat16, jnp.int16
    return pl.pallas_call(
        whole_kernel,
        out_shape=(
            jax.ShapeDtypeStruct((512, B), f32),
            jax.ShapeDtypeStruct((B, R + B), f32),
        ),
        in_specs=[hbm] * 5,
        out_specs=(vmem, vmem),
        scratch_shapes=[
            pltpu.VMEM((1, B), jnp.int32),
            pltpu.VMEM((1, B), jnp.int32),
            pltpu.VMEM((2, 1, 256), f32),
            pltpu.VMEM((512, F), bf16),
            pltpu.VMEM((512, R), f32),
            pltpu.VMEM((512, R), bf16),
            pltpu.VMEM((512, R), bf16),
            pltpu.VMEM((1, 512), f32),
            pltpu.VMEM((B, 128), jnp.int32),
            pltpu.VMEM((16, 128), bf16),
            pltpu.VMEM((32, 128), i16),
            pltpu.VMEM((16, 16, 128), bf16),
            pltpu.VMEM((16, 32, 128), i16),
            pltpu.VMEM((4, 16, 128), bf16),
            pltpu.VMEM((4, 2, 16, 128), i16),
            pltpu.VMEM((3, 16, 128), bf16),
            pltpu.VMEM((3, 2, 16, 128), i16),
            pltpu.VMEM((16, 128), bf16),
            pltpu.VMEM((2, 16, 128), i16),
            pltpu.VMEM((7, 16, 128), bf16),
            pltpu.VMEM((7, 2, 16, 128), i16),
            pltpu.VMEM((2, 4, 8, 16, 128), bf16),
            pltpu.VMEM((2, 4, 8, 2, 16, 128), i16),
            pltpu.VMEM((B, F), bf16),
            pltpu.VMEM((B, R), bf16),
            pltpu.VMEM((B, R), bf16),
            pltpu.VMEM((2, B, 256), f32),
            pltpu.VMEM((10, 4, 8, 8, 128), f32),
            pltpu.VMEM((B, B), f32),
            pltpu.VMEM((B, B), f32),
            pltpu.VMEM((10, 4, 8, 8, 128), f32),
            pltpu.VMEM((5, 4, 8, 8, 128), f32),
            pltpu.VMEM((5, 4, 8, 8, 128), f32),
            pltpu.VMEM((3, 5, 8, 8, 128), f32),
            pltpu.VMEM((5, 8, 8, 128), f32),
            pltpu.VMEM((7, 5, 8, 128), f32),
            pltpu.VMEM((5, 8, 128), f32),
            pltpu.VMEM((8, 5, 8, 128), f32),
            pltpu.SemaphoreType.DMA((8,)),
            pltpu.SemaphoreType.DMA((count,)),
            pltpu.SemaphoreType.DMA((count,)),
        ],
        compiler_params=pltpu.CompilerParams(
            collective_id=0, has_side_effects=True, vmem_limit_bytes=56 * 2**20
        ),
    )(
        pivot_owner.reshape(1, B),
        pivot_position.reshape(1, B),
        ip_weights.reshape(2, 1, 256),
        features,
        factor,
    )


def solution(mesh):
    torus = Mesh(mesh.devices.reshape(4, 8, 2, 8), AXES)
    in_specs = (P(AXES, None), P(AXES, None), P(AXES), P(), P())
    out_specs = (P(AXES, None), P())
    return jax.shard_map(run, mesh=torus, in_specs=in_specs, out_specs=out_specs, check_vma=False)
```

time: 180 us -> 91.7 us (0.51)
  other arithmetic: 61.9 us -> 0 us
  matrix products: 17.5 us -> 0 us
  local copies, waits for them, and re-layouts: 12.9 us -> 4.32 us
  Pallas kernels: 84.5 us -> 86.5 us
    another operation x9 -> x0, other arithmetic: 54.6 us -> none  [the longest x6 34.1 us: body(): lower = jnp.linalg.cholesky(block)]
    dot_general x8 -> x0, matrix products: 14.5 us -> none  [the longest x1 5.31 us: body(): jnp.dot(weighted.T, jnp.concatenate([factor, residual], axis=1), precisio...]
    another operation x9 -> x0, local copies, waits for them, and re-layouts: 5.3 us -> none
    unnamed x8 -> x2, local copies, waits for them, and re-layouts: 0.02 us -> 4.32 us
    gather x2 -> x0, local copies, waits for them, and re-layouts: 3.84 us -> none  [the longest x1 2.16 us: body(): factor[rows] * H_SCALE]
    reduce_sum x4 -> x0, other arithmetic: 3.08 us -> none  [the longest x1 1.22 us: kernel_of(): left_norms = jnp.sum(jnp.square(left.astype(jnp.float32)), axis=1)]
    another operation x5 -> x0, matrix products: 2.99 us -> none  [the longest x2 2.15 us: body(): lower = jnp.linalg.cholesky(block)]
    div x2 -> x0, other arithmetic: 2.49 us -> none  [the longest x1 1.33 us: body(): lower = jnp.linalg.cholesky(block)]
where the time goes in v2:
time: 91.7 us; the launch traced here: 91.4 us
  Pallas kernels  86.5 us (94%)
  local copies, waits for them, and re-layouts  4.32 us (5%)
    pallas_call x1, Pallas kernels, run(): pl.pallas_call(whole_kernel, out_shape=(jax.ShapeDtypeStruct((512, B), f3...  86.5 us
    unnamed x2, local copies, waits for them, and re-layouts  4.32 us

profile of v2, /device:TPU:1, one launch (start us, length us, event | category | flops | bytes accessed | tf_op | source)
XLA Modules:
  0.0 91.4 jit_solution(17219940709582398753)
XLA Ops:
  0.6 86.5 %shard_map.68 = (f32[512,256]{1,0:T(8,128)}, f32[256,1280]{1,0:T(8,128)}) custom-call(s32[1,256]{1,0:T(1,128)} %bitcast.4, s32[1,256]{1,0:T(1,128)} %bitcast.5, f32[2,1,256]{2,1,0:T(1,128)} %bitcast.3, bf16[512,512]{1,0:T(8,128)(2,1)} %features_hbm.1, f32[512,1024]{1,0:T(8,128)} %factor_hbm.1), custom_call_target="tpu_custom_call" | custom-call | tf_op jit(solution)/shard_map/pallas_call | solution.py:442
  87.1 1.9 %copy.9 = f32[512,256]{1,0:T(8,128)} copy(f32[512,256]{1,0:T(8,128)} %get-tuple-element.4) | data formatting | bytes 1048576
  89.0 2.5 %copy.10 = f32[256,1280]{1,0:T(8,128)} copy(f32[256,1280]{1,0:T(8,128)} %get-tuple-element.5) | data formatting | bytes 2621440

commit v3 on v2

--- a/solution.py
+++ b/solution.py
@@ -54,12 +54,11 @@
 Y_PEERS = [dict(y=d) for d in range(1, 8)]
 Z_STEPS = (0, 1, 7, 2, 6, 3, 5, 4)
 Z_PEERS = [dict(z=d) for d in Z_STEPS[1:]]
-ZC_PEERS = [dict(z=d, c=e) for d in Z_STEPS for e in range(2) if (d, e) != (0, 0)]
+XC_PEERS = [dict(x=d, c=e) for d in (0, 1, 3, 2) for e in range(2) if (d, e) != (0, 0)]
 CORE = dict(c=1)
 Z_GROUPS = ((0, 5), (5, 3))
 
 
-CHUNKS = ((0, 3), (3, 2))
 W = 16
 
 
@@ -152,7 +151,8 @@
     owner_hbm, position_hbm, weights_hbm, features_hbm, factor_hbm, columns_out, gram_out,
     owner, position, weights, features, factor, factor_hi, factor_lo, norms, table,
     sx, sh, rx, rh, tx, th, ax, ah, bx, bh, yx, yh, fx, fh,
-    px, pa, pb, rt, m, a, xi, f, cl, a1, xl, a2, zl, a3, yl,
+    px, pa, pb, rt, m, a, xi, f, cl, a1,
+    lx1, sx1, lx2, sx2, lx3, mx1, nx1, mx2, nx2, mx3, lz1, sz1, lz2, sz2, lz3, ly1, sy1, ly2, sy2, ly3,
     load_sem, send_sem, recv_sem,
 ):
     x, z, c, y = (coord(axis) for axis in AXES)
@@ -174,7 +174,7 @@
             pltpu.make_async_copy(factor_hbm.at[rows], factor.at[rows], load_sem.at[1 + i])
         )
         loads[i].start()
-    wait_for_all = greet([peer(**o) for o in ZC_PEERS + X_PEERS + Y_PEERS])
+    wait_for_all = greet([peer(**o) for o in XC_PEERS + Y_PEERS + Z_PEERS])
     sibling = peer(**CORE)
 
     me = ((x * 8 + z) * 2 + c) * 8 + y
@@ -187,8 +187,9 @@
     same = col_owner == row_owner
     row_rank = jnp.sum(jnp.where(same & (i_row < i_col), 1.0, 0.0), axis=0, keepdims=True)
     col_rank = jnp.sum(jnp.where(same & (i_col < i_row), 1.0, 0.0), axis=1, keepdims=True)
-    near = (col_owner[:, :128] // 128 == x) & (col_owner[:, :128] % 8 == y)
-    place = (col_owner[:, :128] // 8) % 16 * 4 + col_rank.astype(jnp.int32)
+    near = col_owner[:, :128] // 128 == x
+    near = near & (col_owner[:, :128] % 8 == y) & ((col_owner[:, :128] // 8) % 2 == c)
+    place = (col_owner[:, :128] // 16) % 8 * 4 + col_rank.astype(jnp.int32)
     table[...] = jnp.where(near, place, -64)
 
     slot = lax.broadcasted_iota(jnp.int32, (48, B), 0)
@@ -221,44 +222,46 @@
     sh[...] = jnp.round(own_h * H_SCALE).astype(jnp.int32).astype(jnp.int16)
 
     wait_for_all()
-    here = z * 2 + c
     pending = []
-    for o in ZC_PEERS:
-        pending.append(copies.start(sx, rx.at[here], peer(**o)))
-        pending.append(copies.start(sh, rh.at[here], peer(**o)))
-    rx[here] = sx[...]
-    rh[here] = sh[...]
+    for o in Z_PEERS:
+        pending.append(copies.start(sx, rx.at[z], peer(**o)))
+        pending.append(copies.start(sh, rh.at[z], peer(**o)))
+    rx[z] = sx[...]
+    rh[z] = sh[...]
     norms[...] = row_norms(features[...])
-    target = table[pl.ds(pl.multiple_of(here * 16, 16), 16), :][:, :1]
+    target = table[pl.ds(pl.multiple_of(z * 32, 32), 32), :][:, :1]
+    halves = [target[:16], target[16:]]
     target_x = jnp.concatenate([target * 4 + b for b in range(4)], axis=0)
-    target_h = jnp.concatenate([target * 8 + b for b in range(8)], axis=0)
+    target_h = jnp.concatenate(
+        [half * 8 + (2 * b + j) for b in range(4) for half in halves for j in range(2)], axis=0
+    )
     pick_x = jnp.where(
-        lax.broadcasted_iota(jnp.int32, (64, 256), 1) == target_x, 1.0, 0.0
+        lax.broadcasted_iota(jnp.int32, (128, 128), 1) == target_x, 1.0, 0.0
     ).astype(jnp.bfloat16)
     pick_h = jnp.where(
-        lax.broadcasted_iota(jnp.int32, (128, 512), 1) == target_h, 1.0, 0.0
+        lax.broadcasted_iota(jnp.int32, (256, 256), 1) == target_h, 1.0, 0.0
     ).astype(jnp.bfloat16)
     for copy in pending:
         copy.wait()
     tx[...] = jnp.dot(
-        pick_x, rx[...].reshape(16 * 16, 128), preferred_element_type=jnp.float32
-    ).astype(jnp.bfloat16).reshape(4, 16, 128)
-    high, low = code_parts(rh[...].reshape(16 * 32, 128))
+        pick_x, rx[...].reshape(8 * 16, 128), preferred_element_type=jnp.float32
+    ).astype(jnp.bfloat16).reshape(4, 2, 16, 128)
+    high, low = code_parts(rh[...].reshape(8 * 32, 128))
     picked = 256.0 * jnp.dot(
         pick_h, high.astype(jnp.bfloat16), preferred_element_type=jnp.float32
     ) + jnp.dot(pick_h, low.astype(jnp.bfloat16), preferred_element_type=jnp.float32)
-    th[...] = picked.astype(jnp.int32).astype(jnp.int16).reshape(4, 2, 16, 128)
+    th[...] = picked.astype(jnp.int32).astype(jnp.int16).reshape(4, 2, 2, 16, 128)
 
     pending = []
-    for i, o in enumerate(X_PEERS):
+    for i, o in enumerate(XC_PEERS):
         device = peer(**o)
-        pending.append(copies.start(tx.at[device[0]], ax.at[i], device))
-        pending.append(copies.start(th.at[device[0]], ah.at[i], device))
+        pending.append(copies.start(tx.at[device[0], device[2]], ax.at[i], device))
+        pending.append(copies.start(th.at[device[0], device[2]], ah.at[i], device))
     for copy in pending:
         copy.wait()
-    total_x = tx[x].astype(jnp.float32)
-    total_h = th[x].astype(jnp.int32)
-    for i in range(3):
+    total_x = tx[x, c].astype(jnp.float32)
+    total_h = th[x, c].astype(jnp.int32)
+    for i in range(7):
         total_x = total_x + ax[i].astype(jnp.float32)
         total_h = total_h + ah[i].astype(jnp.int32)
     bx[...] = total_x.astype(jnp.bfloat16)
@@ -273,31 +276,33 @@
     for i in range(7):
         total_x = total_x + yx[i].astype(jnp.float32)
         total_h = total_h + yh[i].astype(jnp.int32)
-    fx[c, x, 0] = total_x.astype(jnp.bfloat16)
+    fx[c, 0, x] = total_x.astype(jnp.bfloat16)
     fh[c, x, 0] = total_h.astype(jnp.int16)
 
-    along_z = []
-    for i, o in enumerate(Z_PEERS):
-        along_z.append(copies.start(fx.at[c, x, 0], fx.at[c, x, i + 1], peer(**o)))
-        along_z.append(copies.start(fh.at[c, x, 0], fh.at[c, x, i + 1], peer(**o)))
-    along_x, across = [], []
+    x_first = [copies.start(fx.at[c, 0, x], fx.at[c, 0, x], peer(**o)) for o in X_PEERS]
+    z_first = [copies.start(fh.at[c, x, 0], fh.at[c, x, i + 1], peer(**o)) for i, o in enumerate(Z_PEERS)]
+    for copy in x_first:
+        copy.wait_recv()
+    z_second = [copies.start(fx.at[c, 0], fx.at[c, i + 1], peer(**o)) for i, o in enumerate(Z_PEERS)]
+    x_second, across = [], []
     for first, size in Z_GROUPS:
         for i in range(max(first, 1), first + size):
-            along_z[2 * i - 2].wait_recv()
-            along_z[2 * i - 1].wait_recv()
-        part_x, part_h = (ref.at[c, x, pl.ds(first, size)] for ref in (fx, fh))
+            z_first[i - 1].wait_recv()
+        part = fh.at[c, x, pl.ds(first, size)]
         for o in X_PEERS:
-            along_x.append(copies.start(part_x, part_x, peer(**o)))
-            along_x.append(copies.start(part_h, part_h, peer(**o)))
-        across.append(copies.start(part_x, part_x, sibling))
-        across.append(copies.start(part_h, part_h, sibling))
+            x_second.append(copies.start(part, part, peer(**o)))
+        across.append(copies.start(part, part, sibling))
+    for first, size in Z_GROUPS:
+        for i in range(max(first, 1), first + size):
+            z_second[i - 1].wait_recv()
+        part = fx.at[c, pl.ds(first, size)]
+        across.append(copies.start(part, part, sibling))
     for g, (first, size) in enumerate(Z_GROUPS):
         for i, o in enumerate(X_PEERS):
             source = lax.rem(x + 4 - o["x"], 4)
-            for j, ref in enumerate((fx, fh)):
-                part = ref.at[c, source, pl.ds(first, size)]
-                along_x[(g * 3 + i) * 2 + j].wait_recv()
-                across.append(copies.start(part, part, sibling))
+            part = fh.at[c, source, pl.ds(first, size)]
+            x_second[g * 3 + i].wait_recv()
+            across.append(copies.start(part, part, sibling))
 
     def unpack(core):
         def step(i, carry):
@@ -305,7 +310,7 @@
             back = odd * ((i + 1) // 2) + (1 - odd) * (8 - i // 2)
             rows = pl.ds(pl.multiple_of((((z + 8 - back) % 8) * 2 + core) * 16, 16), 16)
             for xb in range(4):
-                px[rows, xb * 128 : xb * 128 + 128] = fx[core, xb, i]
+                px[rows, xb * 128 : xb * 128 + 128] = fx[core, i, xb]
                 for j in range(2):
                     high, low = code_parts(fh[core, xb, i, j])
                     at = (xb * 2 + j) * 128
@@ -316,7 +321,7 @@
         lax.fori_loop(0, 8, step, 0)
 
     unpack(c)
-    for copy in along_z + along_x:
+    for copy in x_first + z_first + z_second + x_second:
         copy.wait_send()
     for copy in across:
         copy.wait()
@@ -340,46 +345,101 @@
     m[...] = jnp.zeros_like(m)
     lax.fori_loop(0, 2, local, 0)
 
-    def core_out(o, n):
-        return [copies.start(m.at[pl.ds(5 * (1 - c) + o, n)], cl.at[pl.ds(o, n)], sibling)]
-
-    def core_in(o, n):
-        a1[o : o + n] = m[pl.ds(5 * c + o, n)] + cl[o : o + n]
-
-    def x_out(o, n):
-        return [
-            copies.start(a1.at[pl.ds(o, n), peer(**p)[0]], xl.at[i, pl.ds(o, n)], peer(**p))
-            for i, p in enumerate(X_PEERS)
-        ]
-
-    def x_in(o, n):
-        a2[o : o + n] = a1[o : o + n, x] + xl[0, o : o + n] + xl[1, o : o + n] + xl[2, o : o + n]
-
-    def z_out(o, n):
-        return [
-            copies.start(a2.at[pl.ds(o, n), peer(**p)[1]], zl.at[i, pl.ds(o, n)], peer(**p))
-            for i, p in enumerate(Z_PEERS)
-        ]
-
-    def z_in(o, n):
-        total = a2[o : o + n, z]
-        for i in range(7):
-            total = total + zl[i, o : o + n]
-        a3[o : o + n] = total
-        yl[y, o : o + n] = total
-
-    def y_out(o, n):
-        return [copies.start(a3.at[pl.ds(o, n)], yl.at[y, pl.ds(o, n)], peer(**p)) for p in Y_PEERS]
-
-    def y_in(o, n):
-        total = yl[0, o : o + n]
-        for i in range(1, 8):
-            total = total + yl[i, o : o + n]
-        f[pl.ds(5 * c + o, n), x, z] = total
-
-    def back(o, n, place, peers):
-        block = f.at[(pl.ds(5 * c + o, n), *place)]
-        return [copies.start(block, block, peer(**p)) for p in peers]
+    axis_at = dict(x=x, y=y, z=z)
+    axis_peers = dict(x=X_PEERS, y=Y_PEERS, z=Z_PEERS)
+
+    class Chunk:
+        def __init__(self, o, n, first, second, last, land1, sum1, land2, sum2, land3):
+            self.o, self.n = o, n
+            self.first, self.second, self.last = first, second, last
+            self.land1, self.sum1, self.land2, self.sum2, self.land3 = land1, sum1, land2, sum2, land3
+            self.wide = second if first == "x" else first
+            self.flying = []
+
+        def line(self, ref, start, along, index):
+            block = (pl.ds(start, self.n),)
+            return ref.at[block + ((index,) if along == "x" else (slice(None), index))]
+
+        def go(self, pairs):
+            self.flying = [copies.start(source, target, device) for source, target, device in pairs]
+
+        def land(self):
+            for copy in self.flying:
+                copy.wait()
+
+        def targets(self, axis):
+            where = AXES.index(axis)
+            return [(i, peer(**o)[where], peer(**o)) for i, o in enumerate(axis_peers[axis])]
+
+        def core_out(self):
+            theirs = m.at[pl.ds(5 * (1 - c) + self.o, self.n)]
+            self.go([(theirs, cl.at[pl.ds(self.o, self.n)], sibling)])
+
+        def first_out(self):
+            self.land()
+            span = pl.ds(self.o, self.n)
+            a1[span] = m[pl.ds(5 * c + self.o, self.n)] + cl[span]
+            self.go([
+                (self.line(a1, self.o, self.first, at), self.land1.at[i], device)
+                for i, at, device in self.targets(self.first)
+            ])
+
+        def second_out(self):
+            self.land()
+            total = self.line(a1, self.o, self.first, axis_at[self.first])[...]
+            for i in range(len(axis_peers[self.first])):
+                total = total + self.land1[i]
+            self.sum1[...] = total
+            self.go([
+                (self.sum1.at[:, at], self.land2.at[i], device)
+                for i, at, device in self.targets(self.second)
+            ])
+
+        def last_out(self):
+            self.land()
+            total = self.sum1[:, axis_at[self.second]]
+            for i in range(len(axis_peers[self.second])):
+                total = total + self.land2[i]
+            self.sum2[...] = total
+            here = self.land3.at[axis_at[self.last]]
+            here[...] = total
+            self.go([(self.sum2, here, device) for _, _, device in self.targets(self.last)])
+
+        def second_back(self):
+            self.land()
+            total = self.land3[0]
+            for i in range(1, 8):
+                total = total + self.land3[i]
+            block = f.at[pl.ds(5 * c + self.o, self.n), x, axis_at[self.wide]]
+            block[...] = total
+            self.go([(block, block, device) for _, _, device in self.targets(self.second)])
+
+        def first_back(self):
+            self.land()
+            block = self.line(f, 5 * c + self.o, self.first, axis_at[self.first])
+            self.go([(block, block, device) for _, _, device in self.targets(self.first)])
+
+        def core_back(self):
+            if self.first != "x":
+                self.land()
+                block = f.at[pl.ds(5 * c + self.o, self.n)]
+                self.go([(block, block, sibling)])
+                return
+            sent = self.flying
+            block = self.line(f, 5 * c + self.o, "x", x)
+            pairs = [copies.start(block, block, sibling)]
+            for copy, o in zip(sent, X_PEERS):
+                copy.wait_recv()
+                block = self.line(f, 5 * c + self.o, "x", lax.rem(x + 4 - o["x"], 4))
+                pairs.append(copies.start(block, block, sibling))
+            for copy in sent:
+                copy.wait_send()
+            self.flying = pairs
+
+    cx1 = Chunk(0, 2, "x", "z", "y", lx1, sx1, lx2, sx2, lx3)
+    cx2 = Chunk(2, 1, "x", "z", "y", mx1, nx1, mx2, nx2, mx3)
+    cz = Chunk(3, 1, "z", "x", "y", lz1, sz1, lz2, sz2, lz3)
+    cy = Chunk(4, 1, "y", "x", "z", ly1, sy1, ly2, sy2, ly3)
 
     def begin_block():
         h = [pa[...], pb[...]]
@@ -392,50 +452,60 @@
         flipped = product(split(xi[...], 3), split(rt[i], 3), (1, 0), 3)
         columns_out[i * 256 : (i + 1) * 256, :] = flipped.T
 
-    beside = [
-        [begin_block, lambda: eliminate(0, 2, a, xi)],
-        [lambda: eliminate(2, 8, a, xi)],
-        [lambda: eliminate(8, 12, a, xi)],
-        [lambda: eliminate(12, 16, a, xi)],
-        [lambda: columns_of(0)],
-        [lambda: columns_of(1)],
-        [],
-    ]
-    stages = [
-        (core_out, core_in),
-        (x_out, x_in),
-        (z_out, z_in),
-        (y_out, y_in),
-        (lambda o, n: back(o, n, (x, z), Z_PEERS), None),
-        (lambda o, n: back(o, n, (x,), X_PEERS), None),
-        (lambda o, n: back(o, n, (), [CORE]), None),
-    ]
-    flying = {chunk: stages[0][0](*chunk) for chunk in CHUNKS}
-    for s in range(len(stages)):
-        for work in beside[s]:
-            work()
-        for chunk in CHUNKS:
-            for copy in flying[chunk]:
-                copy.wait()
-            if stages[s][1] is not None:
-                stages[s][1](*chunk)
-            if s + 1 < len(stages):
-                flying[chunk] = stages[s + 1][0](*chunk)
+    for chunk in (cz, cy, cx1, cx2):
+        chunk.core_out()
+    for chunk in (cz, cy, cx1, cx2):
+        chunk.first_out()
+    begin_block()
+    eliminate(0, 5, a, xi)
+    for chunk in (cx1, cz, cy, cx2):
+        chunk.second_out()
+    eliminate(5, 8, a, xi)
+    for chunk in (cz, cy, cx1, cx2):
+        chunk.last_out()
+    eliminate(8, 16, a, xi)
+    for chunk in (cz, cy, cx1, cx2):
+        chunk.second_back()
+    columns_of(0)
+    for chunk in (cz, cy, cx1, cx2):
+        chunk.first_back()
+    columns_of(1)
+    for chunk in (cz, cy, cx1, cx2):
+        chunk.core_back()
 
     inverse = split(xi[...], 3)
     scaled = 1.0 / (512 * 512)
 
-    def total_of(k):
-        return jnp.concatenate([f[k].reshape(B, 128), f[k + 1].reshape(B, 128)], axis=1)
-
-    for k in range(0, 8, 2):
-        gram_out[:, k * 128 : k * 128 + 256] = scaled * product(inverse, split(total_of(k), 3), (1, 0), 3)
-    right = product(inverse, split(total_of(8), 3), (1, 0), 3)
-    gram_out[:, R:] = scaled * product(split(right, 3), inverse, (1, 1), 3)
+    def applied(*blocks):
+        total = jnp.concatenate([f[k].reshape(B, 128) for k in blocks], axis=1)
+        return product(inverse, split(total, 3), (1, 0), 3)
+
+    cz.land()
+    cy.land()
+    gram_out[:, 3 * 128 : 5 * 128] = scaled * applied(3, 4)
+    gram_out[:, R:] = scaled * product(split(applied(8, 9), 3), inverse, (1, 1), 3)
+    cx1.land()
+    gram_out[:, :256] = scaled * applied(0, 1)
+    gram_out[:, 5 * 128 : 7 * 128] = scaled * applied(5, 6)
+    cx2.land()
+    last = scaled * applied(2, 7)
+    gram_out[:, 2 * 128 : 3 * 128] = last[:, :128]
+    gram_out[:, 7 * 128 : 8 * 128] = last[:, 128:]
+
+
+def sum_buffers(n, first, second):
+    shapes = [
+        (first, n, second, 8, 128),
+        (n, second, 8, 128),
+        (second - 1, n, 8, 128),
+        (n, 8, 128),
+        (8, n, 8, 128),
+    ]
+    return [pltpu.VMEM(shape, jnp.float32) for shape in shapes]
 
 
 def run(features, factor, ip_weights, pivot_owner, pivot_position):
-    count = 92 + len(CHUNKS) * 29
+    count = 64 + 16 + 4 * 32
     vmem = pl.BlockSpec(memory_space=pltpu.VMEM)
     hbm = pl.BlockSpec(memory_space=pltpu.HBM)
     f32, bf16, i16 = jnp.float32, jnp.bfloat16, jnp.int16
@@ -459,17 +529,17 @@
             pltpu.VMEM((B, 128), jnp.int32),
             pltpu.VMEM((16, 128), bf16),
             pltpu.VMEM((32, 128), i16),
-            pltpu.VMEM((16, 16, 128), bf16),
-            pltpu.VMEM((16, 32, 128), i16),
-            pltpu.VMEM((4, 16, 128), bf16),
-            pltpu.VMEM((4, 2, 16, 128), i16),
-            pltpu.VMEM((3, 16, 128), bf16),
-            pltpu.VMEM((3, 2, 16, 128), i16),
+            pltpu.VMEM((8, 16, 128), bf16),
+            pltpu.VMEM((8, 32, 128), i16),
+            pltpu.VMEM((4, 2, 16, 128), bf16),
+            pltpu.VMEM((4, 2, 2, 16, 128), i16),
+            pltpu.VMEM((7, 16, 128), bf16),
+            pltpu.VMEM((7, 2, 16, 128), i16),
             pltpu.VMEM((16, 128), bf16),
             pltpu.VMEM((2, 16, 128), i16),
             pltpu.VMEM((7, 16, 128), bf16),
             pltpu.VMEM((7, 2, 16, 128), i16),
-            pltpu.VMEM((2, 4, 8, 16, 128), bf16),
+            pltpu.VMEM((2, 8, 4, 16, 128), bf16),
             pltpu.VMEM((2, 4, 8, 2, 16, 128), i16),
             pltpu.VMEM((B, F), bf16),
             pltpu.VMEM((B, R), bf16),
@@ -481,11 +551,10 @@
             pltpu.VMEM((10, 4, 8, 8, 128), f32),
             pltpu.VMEM((5, 4, 8, 8, 128), f32),
             pltpu.VMEM((5, 4, 8, 8, 128), f32),
-            pltpu.VMEM((3, 5, 8, 8, 128), f32),
-            pltpu.VMEM((5, 8, 8, 128), f32),
-            pltpu.VMEM((7, 5, 8, 128), f32),
-            pltpu.VMEM((5, 8, 128), f32),
-            pltpu.VMEM((8, 5, 8, 128), f32),
+            *sum_buffers(2, 3, 8),
+            *sum_buffers(1, 3, 8),
+            *sum_buffers(1, 7, 4),
+            *sum_buffers(1, 7, 4),
             pltpu.SemaphoreType.DMA((8,)),
             pltpu.SemaphoreType.DMA((count,)),
             pltpu.SemaphoreType.DMA((count,)),

time: 91.7 us -> 85.7 us (0.935)
  Pallas kernels: 86.5 us -> 80.5 us
    pallas_call x1, Pallas kernels: 86.5 us -> 80.5 us  [run(): pl.pallas_call(whole_kernel, out_shape=(jax.ShapeDtypeStruct((512, B), f3...]
where the time goes in v3:
time: 85.7 us; the launch traced here: 85.4 us
  Pallas kernels  80.5 us (94%)
  local copies, waits for them, and re-layouts  4.32 us (5%)
    pallas_call x1, Pallas kernels, run(): pl.pallas_call(whole_kernel, out_shape=(jax.ShapeDtypeStruct((512, B), f3...  80.5 us
    unnamed x2, local copies, waits for them, and re-layouts  4.32 us

profile of v3, /device:TPU:1, one launch (start us, length us, event | category | flops | bytes accessed | tf_op | source)
XLA Modules:
  0.0 85.4 jit_solution(10187659038269073903)
XLA Ops:
  0.6 80.5 %shard_map.68 = (f32[512,256]{1,0:T(8,128)}, f32[256,1280]{1,0:T(8,128)}) custom-call(s32[1,256]{1,0:T(1,128)} %bitcast.4, s32[1,256]{1,0:T(1,128)} %bitcast.5, f32[2,1,256]{2,1,0:T(1,128)} %bitcast.3, bf16[512,512]{1,0:T(8,128)(2,1)} %features_hbm.1, f32[512,1024]{1,0:T(8,128)} %factor_hbm.1), custom_call_target="tpu_custom_call" | custom-call | tf_op jit(solution)/shard_map/pallas_call | solution.py:512
  81.1 1.9 %copy.9 = f32[512,256]{1,0:T(8,128)} copy(f32[512,256]{1,0:T(8,128)} %get-tuple-element.4) | data formatting | bytes 1048576
  83.0 2.5 %copy.10 = f32[256,1280]{1,0:T(8,128)} copy(f32[256,1280]{1,0:T(8,128)} %get-tuple-element.5) | data formatting | bytes 2621440

commit v4 on v3

--- a/solution.py
+++ b/solution.py
@@ -50,11 +50,11 @@
     return lambda: pl.semaphore_wait(barrier, len(peers))
 
 
-X_PEERS = [dict(x=d) for d in (1, 3, 2)]
-Y_PEERS = [dict(y=d) for d in range(1, 8)]
-Z_STEPS = (0, 1, 7, 2, 6, 3, 5, 4)
-Z_PEERS = [dict(z=d) for d in Z_STEPS[1:]]
-XC_PEERS = [dict(x=d, c=e) for d in (0, 1, 3, 2) for e in range(2) if (d, e) != (0, 0)]
+X_PEERS = [dict(x=d) for d in (2, 1, 3)]
+Y_PEERS = [dict(y=d) for d in (4, 3, 5, 2, 6, 1, 7)]
+Z_PEERS = [dict(z=d) for d in (4, 3, 5, 2, 6, 1, 7)]
+XC_PEERS = [dict(x=d, c=e) for d in (2, 1, 3, 0) for e in (1, 0) if (d, e) != (0, 0)]
+Z_ORDER = [dict(z=d) for d in (1, 7, 2, 6, 3, 5, 4)]
 CORE = dict(c=1)
 Z_GROUPS = ((0, 5), (5, 3))
 
@@ -192,33 +192,26 @@
     place = (col_owner[:, :128] // 16) % 8 * 4 + col_rank.astype(jnp.int32)
     table[...] = jnp.where(near, place, -64)
 
-    slot = lax.broadcasted_iota(jnp.int32, (48, B), 0)
-    slot = jnp.where(slot < 16, slot // 4, (slot - 16) // 8)
-    mine = (row_owner == me) & (row_rank.astype(jnp.int32) == slot)
-    at = jnp.sum(
-        jnp.where(mine, position[...].astype(jnp.float32) + 1.0, 0.0), axis=1, keepdims=True
-    ).astype(jnp.int32) - 1
-    pick = jnp.where(lax.broadcasted_iota(jnp.int32, (48, 512), 1) == at, 1.0, 0.0).astype(jnp.bfloat16)
+    order = row_rank.astype(jnp.int32)
+    spots = [
+        jnp.sum(jnp.where((row_owner == me) & (order == s), position[...], 0)) for s in range(4)
+    ]
+    slot = lax.broadcasted_iota(jnp.int32, (16, 512), 0) // 4
+    lane = lax.broadcasted_iota(jnp.int32, (16, 512), 1)
+    wanted = jnp.where(slot == 0, spots[0], jnp.where(slot == 1, spots[1], jnp.where(slot == 2, spots[2], spots[3])))
+    pick = jnp.where(lane == wanted, 1.0, 0.0).astype(jnp.bfloat16)
     load_x.wait()
-    rows_x = jnp.dot(pick[:16], features[...], preferred_element_type=jnp.float32)
+    rows_x = jnp.dot(pick, features[...], preferred_element_type=jnp.float32)
     block_x = lax.broadcasted_iota(jnp.int32, (16, 128), 0) % 4
     sx[...] = sum(
         jnp.where(block_x == b, rows_x[:, b * 128 : b * 128 + 128], 0.0) for b in range(4)
     ).astype(jnp.bfloat16)
     for load in loads:
         load.wait()
-
-    def cut(i, carry):
-        rows = pl.ds(pl.multiple_of(i * 64, 64), 64)
-        factor_hi[rows, :], factor_lo[rows, :] = split(factor[rows, :], 2)
-        return carry
-
-    lax.fori_loop(0, 8, cut, 0)
-    rows_h = jnp.dot(pick[16:], factor_hi[...], preferred_element_type=jnp.float32) + jnp.dot(
-        pick[16:], factor_lo[...], preferred_element_type=jnp.float32
-    )
-    block_h = lax.broadcasted_iota(jnp.int32, (32, 128), 0) % 8
-    own_h = sum(jnp.where(block_h == b, rows_h[:, b * 128 : b * 128 + 128], 0.0) for b in range(8))
+    rows_h = [factor[pl.ds(spot, 1), :] for spot in spots]
+    own_h = jnp.concatenate(
+        [row[:, b * 128 : b * 128 + 128] for row in rows_h for b in range(8)], axis=0
+    )
     sh[...] = jnp.round(own_h * H_SCALE).astype(jnp.int32).astype(jnp.int16)
 
     wait_for_all()
@@ -228,6 +221,13 @@
         pending.append(copies.start(sh, rh.at[z], peer(**o)))
     rx[z] = sx[...]
     rh[z] = sh[...]
+
+    def cut(i, carry):
+        rows = pl.ds(pl.multiple_of(i * 64, 64), 64)
+        factor_hi[rows, :], factor_lo[rows, :] = split(factor[rows, :], 2)
+        return carry
+
+    lax.fori_loop(0, 8, cut, 0)
     norms[...] = row_norms(features[...])
     target = table[pl.ds(pl.multiple_of(z * 32, 32), 32), :][:, :1]
     halves = [target[:16], target[16:]]
@@ -280,10 +280,14 @@
     fh[c, x, 0] = total_h.astype(jnp.int16)
 
     x_first = [copies.start(fx.at[c, 0, x], fx.at[c, 0, x], peer(**o)) for o in X_PEERS]
-    z_first = [copies.start(fh.at[c, x, 0], fh.at[c, x, i + 1], peer(**o)) for i, o in enumerate(Z_PEERS)]
+    z_first = [
+        copies.start(fh.at[c, x, 0], fh.at[c, x, 7 - i], peer(**o)) for i, o in enumerate(Z_ORDER[::-1])
+    ][::-1]
     for copy in x_first:
         copy.wait_recv()
-    z_second = [copies.start(fx.at[c, 0], fx.at[c, i + 1], peer(**o)) for i, o in enumerate(Z_PEERS)]
+    z_second = [
+        copies.start(fx.at[c, 0], fx.at[c, 7 - i], peer(**o)) for i, o in enumerate(Z_ORDER[::-1])
+    ][::-1]
     x_second, across = [], []
     for first, size in Z_GROUPS:
         for i in range(max(first, 1), first + size):
@@ -298,7 +302,7 @@
         part = fx.at[c, pl.ds(first, size)]
         across.append(copies.start(part, part, sibling))
     for g, (first, size) in enumerate(Z_GROUPS):
-        for i, o in enumerate(X_PEERS):
+        for i, o in list(enumerate(X_PEERS))[::-1]:
             source = lax.rem(x + 4 - o["x"], 4)
             part = fh.at[c, source, pl.ds(first, size)]
             x_second[g * 3 + i].wait_recv()
@@ -428,7 +432,7 @@
             sent = self.flying
             block = self.line(f, 5 * c + self.o, "x", x)
             pairs = [copies.start(block, block, sibling)]
-            for copy, o in zip(sent, X_PEERS):
+            for copy, o in list(zip(sent, X_PEERS))[::-1]:
                 copy.wait_recv()
                 block = self.line(f, 5 * c + self.o, "x", lax.rem(x + 4 - o["x"], 4))
                 pairs.append(copies.start(block, block, sibling))
@@ -512,8 +516,8 @@
     return pl.pallas_call(
         whole_kernel,
         out_shape=(
-            jax.ShapeDtypeStruct((512, B), f32),
-            jax.ShapeDtypeStruct((B, R + B), f32),
+            pltpu.VMEM((512, B), f32),
+            pltpu.VMEM((B, R + B), f32),
         ),
         in_specs=[hbm] * 5,
         out_specs=(vmem, vmem),
@@ -560,14 +564,11 @@
             pltpu.SemaphoreType.DMA((count,)),
         ],
         compiler_params=pltpu.CompilerParams(
-            collective_id=0, has_side_effects=True, vmem_limit_bytes=56 * 2**20
+            collective_id=0, has_side_effects=True, vmem_limit_bytes=48 * 2**20
         ),
     )(
-        pivot_owner.reshape(1, B),
-        pivot_position.reshape(1, B),
-        ip_weights.reshape(2, 1, 256),
-        features,
-        factor,
+        *(pltpu.with_memory_space_constraint(v, pltpu.HBM) for v in (
+            pivot_owner.reshape(1, B), pivot_position.reshape(1, B), ip_weights.reshape(2, 1, 256), features, factor)),
     )
 
 

time: 85.7 us -> 80.3 us (0.937)
  Pallas kernels: 80.5 us -> 77.6 us
  local copies, waits for them, and re-layouts: 4.32 us -> 1.85 us
    pallas_call x1, Pallas kernels: 80.5 us -> 77.6 us  [run(): pl.pallas_call(whole_kernel, out_shape=(pltpu.VMEM((512, B), f32), pltpu....]
    unnamed x2, local copies, waits for them, and re-layouts: 4.32 us -> 1.85 us
where the time goes in v4:
time: 80.3 us; the launch traced here: 80.1 us
  Pallas kernels  77.6 us (97%)
  local copies, waits for them, and re-layouts  1.85 us (2%)
    pallas_call x1, Pallas kernels, run(): pl.pallas_call(whole_kernel, out_shape=(pltpu.VMEM((512, B), f32), pltpu....  77.6 us
    unnamed x2, local copies, waits for them, and re-layouts  1.85 us

profile of v4, /device:TPU:1, one launch (start us, length us, event | category | flops | bytes accessed | tf_op | source)
XLA Modules:
  0.0 80.1 jit_solution(13623716146687903319)
XLA Ops:
  0.6 77.6 %shard_map.68 = (f32[512,256]{1,0:T(8,128)S(1)}, f32[256,1280]{1,0:T(8,128)S(1)}) custom-call(s32[1,256]{1,0:T(1,128)} %bitcast.4, s32[1,256]{1,0:T(1,128)} %bitcast.5, f32[2,1,256]{2,1,0:T(1,128)} %bitcast.3, bf16[512,512]{1,0:T(8,128)(2,1)} %features_hbm.1, f32[512,1024]{1,0:T(8,128)} %factor_hbm.1), custom_call_target="tpu_custom_call" | custom-call | tf_op jit(solution)/shard_map/pallas_call | solution.py:516
  78.3 0.8 copy.9
  79.1 1.1 %copy.10 = f32[256,1280]{1,0:T(8,128)} copy(f32[256,1280]{1,0:T(8,128)S(1)} %get-tuple-element.3) | data formatting | bytes 2621440

commit v5 on v4

--- a/solution.py
+++ b/solution.py
@@ -151,7 +151,7 @@
     owner_hbm, position_hbm, weights_hbm, features_hbm, factor_hbm, columns_out, gram_out,
     owner, position, weights, features, factor, factor_hi, factor_lo, norms, table,
     sx, sh, rx, rh, tx, th, ax, ah, bx, bh, yx, yh, fx, fh,
-    px, pa, pb, rt, m, a, xi, f, cl, a1,
+    px, pa, pb, rt, rest_hi, rest_lo, weighted_hi, weighted_lo, m, a, xi, f, cl, a1,
     lx1, sx1, lx2, sx2, lx3, mx1, nx1, mx2, nx2, mx3, lz1, sz1, lz2, sz2, lz3, ly1, sy1, ly2, sy2, ly3,
     load_sem, send_sem, recv_sem,
 ):
@@ -338,16 +338,27 @@
             [pa[...], pb[...]], h, (1, 1), 2
         )
         rt[i] = residual
-        weighted = split(residual * weights[i], 2)
-        left = product(weighted, h, (1, 0), 2)
-        right = product(weighted, split(residual, 2), (1, 1), 2)
-        both = jnp.concatenate([left, right], axis=1)
-        for k in range(10):
-            m[k] = m[k] + both[:, k * 128 : k * 128 + 128].reshape(4, 8, 8, 128)
+        rest_hi[:, span], rest_lo[:, span] = split(residual, 2)
+        weighted_hi[:, span], weighted_lo[:, span] = split(residual * weights[i], 2)
         return carry
 
-    m[...] = jnp.zeros_like(m)
     lax.fori_loop(0, 2, local, 0)
+
+    def share(half):
+        weighted = [weighted_hi[...], weighted_lo[...]]
+        lanes = slice(0, 640) if half == 0 else slice(640, R)
+        values = product(weighted, [factor_hi[:, lanes], factor_lo[:, lanes]], (1, 0), 2)
+        if half == 1:
+            right = product(weighted, [rest_hi[...], rest_lo[...]], (1, 1), 2)
+            values = jnp.concatenate([values, right], axis=1)
+        for k in range(5):
+            m[5 * half + k] = values[:, k * 128 : k * 128 + 128].reshape(4, 8, 8, 128)
+
+    def share_when(core, half):
+        pl.when(c == core)(lambda: share(half))
+
+    share_when(0, 1)
+    share_when(1, 0)
 
     axis_at = dict(x=x, y=y, z=z)
     axis_peers = dict(x=X_PEERS, y=Y_PEERS, z=Z_PEERS)
@@ -458,6 +469,8 @@
 
     for chunk in (cz, cy, cx1, cx2):
         chunk.core_out()
+    share_when(0, 0)
+    share_when(1, 1)
     for chunk in (cz, cy, cx1, cx2):
         chunk.first_out()
     begin_block()
@@ -513,7 +526,7 @@
     vmem = pl.BlockSpec(memory_space=pltpu.VMEM)
     hbm = pl.BlockSpec(memory_space=pltpu.HBM)
     f32, bf16, i16 = jnp.float32, jnp.bfloat16, jnp.int16
-    return pl.pallas_call(
+    results = pl.pallas_call(
         whole_kernel,
         out_shape=(
             pltpu.VMEM((512, B), f32),
@@ -549,6 +562,10 @@
             pltpu.VMEM((B, R), bf16),
             pltpu.VMEM((B, R), bf16),
             pltpu.VMEM((2, B, 256), f32),
+            pltpu.VMEM((B, 512), bf16),
+            pltpu.VMEM((B, 512), bf16),
+            pltpu.VMEM((B, 512), bf16),
+            pltpu.VMEM((B, 512), bf16),
             pltpu.VMEM((10, 4, 8, 8, 128), f32),
             pltpu.VMEM((B, B), f32),
             pltpu.VMEM((B, B), f32),
@@ -570,6 +587,27 @@
         *(pltpu.with_memory_space_constraint(v, pltpu.HBM) for v in (
             pivot_owner.reshape(1, B), pivot_position.reshape(1, B), ip_weights.reshape(2, 1, 256), features, factor)),
     )
+    vmem = pl.BlockSpec(memory_space=pltpu.VMEM)
+    return pl.pallas_call(
+        write_kernel,
+        out_shape=(pltpu.HBM((512, B), f32), pltpu.HBM((B, R + B), f32)),
+        in_specs=[vmem, vmem],
+        out_specs=(hbm, hbm),
+        scratch_shapes=[pltpu.SemaphoreType.DMA((3,))],
+        compiler_params=pltpu.CompilerParams(vmem_limit_bytes=2**20),
+    )(*results)
+
+
+def write_kernel(columns, gram, columns_out, gram_out, sem):
+    copies = [
+        pltpu.make_async_copy(columns, columns_out, sem.at[0]),
+        pltpu.make_async_copy(gram.at[pl.ds(0, 128)], gram_out.at[pl.ds(0, 128)], sem.at[1]),
+        pltpu.make_async_copy(gram.at[pl.ds(128, 128)], gram_out.at[pl.ds(128, 128)], sem.at[2]),
+    ]
+    for copy in copies:
+        copy.start()
+    for copy in copies:
+        copy.wait()
 
 
 def solution(mesh):

time: 80.3 us -> 78 us (0.971)
  local copies, waits for them, and re-layouts: 1.85 us -> 0 us
    unnamed x2 -> x0, local copies, waits for them, and re-layouts: 1.85 us -> none
    pallas_call x1, Pallas kernels: 77.6 us -> 75.9 us  [run(): pl.pallas_call(whole_kernel, out_shape=(pltpu.VMEM((512, B), f32), pltpu....]
    pallas_call x0 -> x1, Pallas kernels: none -> 1.25 us  [run(): pl.pallas_call(write_kernel, out_shape=(pltpu.HBM((512, B), f32), pltpu.H...]
where the time goes in v5:
time: 78 us; the launch traced here: 77.8 us
  Pallas kernels  77.2 us (99%)
    pallas_call x1, Pallas kernels, run(): pl.pallas_call(whole_kernel, out_shape=(pltpu.VMEM((512, B), f32), pltpu....  75.9 us

profile of v5, /device:TPU:1, one launch (start us, length us, event | category | flops | bytes accessed | tf_op | source)
XLA Modules:
  0.0 77.8 jit_solution(5084873969113446545)
XLA Ops:
  0.6 75.9 %shard_map.68 = (f32[512,256]{1,0:T(8,128)S(1)}, f32[256,1280]{1,0:T(8,128)S(1)}) custom-call(s32[1,256]{1,0:T(1,128)} %bitcast.4, s32[1,256]{1,0:T(1,128)} %bitcast.5, f32[2,1,256]{2,1,0:T(1,128)} %bitcast.3, bf16[512,512]{1,0:T(8,128)(2,1)} %features_hbm.1, f32[512,1024]{1,0:T(8,128)} %factor_hbm.1), custom_call_target="tpu_custom_call" | custom-call | tf_op jit(solution)/shard_map/pallas_call | solution.py:529
  76.6 1.3 %shard_map.69 = (f32[512,256]{1,0:T(8,128)}, f32[256,1280]{1,0:T(8,128)}) custom-call(f32[512,256]{1,0:T(8,128)S(1)} %get-tuple-element.4.columns, f32[256,1280]{1,0:T(8,128)S(1)} %get-tuple-element.5.gram), custom_call_target="tpu_custom_call" | custom-call | tf_op jit(solution)/shard_map/pallas_call | solution.py:591

commit v6 on v5

--- a/solution.py
+++ b/solution.py
@@ -157,6 +157,7 @@
 ):
     x, z, c, y = (coord(axis) for axis in AXES)
     copies = Copies(send_sem, recv_sem)
+    wait_for_all = greet([peer(**o) for o in Z_PEERS + Y_PEERS + XC_PEERS])
     small = [
         pltpu.make_async_copy(source, target, load_sem.at[5 + i])
         for i, (source, target) in enumerate(
@@ -174,7 +175,6 @@
             pltpu.make_async_copy(factor_hbm.at[rows], factor.at[rows], load_sem.at[1 + i])
         )
         loads[i].start()
-    wait_for_all = greet([peer(**o) for o in XC_PEERS + Y_PEERS + Z_PEERS])
     sibling = peer(**CORE)
 
     me = ((x * 8 + z) * 2 + c) * 8 + y
@@ -241,7 +241,7 @@
     pick_h = jnp.where(
         lax.broadcasted_iota(jnp.int32, (256, 256), 1) == target_h, 1.0, 0.0
     ).astype(jnp.bfloat16)
-    for copy in pending:
+    for copy in pending[::-1]:
         copy.wait()
     tx[...] = jnp.dot(
         pick_x, rx[...].reshape(8 * 16, 128), preferred_element_type=jnp.float32
@@ -257,7 +257,7 @@
         device = peer(**o)
         pending.append(copies.start(tx.at[device[0], device[2]], ax.at[i], device))
         pending.append(copies.start(th.at[device[0], device[2]], ah.at[i], device))
-    for copy in pending:
+    for copy in pending[::-1]:
         copy.wait()
     total_x = tx[x, c].astype(jnp.float32)
     total_h = th[x, c].astype(jnp.int32)
@@ -271,7 +271,7 @@
     for i, o in enumerate(Y_PEERS):
         pending.append(copies.start(bx, yx.at[i], peer(**o)))
         pending.append(copies.start(bh, yh.at[i], peer(**o)))
-    for copy in pending:
+    for copy in pending[::-1]:
         copy.wait()
     for i in range(7):
         total_x = total_x + yx[i].astype(jnp.float32)
@@ -379,7 +379,7 @@
             self.flying = [copies.start(source, target, device) for source, target, device in pairs]
 
         def land(self):
-            for copy in self.flying:
+            for copy in self.flying[::-1]:
                 copy.wait()
 
         def targets(self, axis):

time: 78 us -> 76.5 us (0.981)
  Pallas kernels: 77.2 us -> 75.7 us
    pallas_call x1, Pallas kernels: 75.9 us -> 74.4 us  [run(): pl.pallas_call(whole_kernel, out_shape=(pltpu.VMEM((512, B), f32), pltpu....]
where the time goes in v6:
time: 76.5 us; the launch traced here: 76.3 us
  Pallas kernels  75.7 us (99%)
    pallas_call x1, Pallas kernels, run(): pl.pallas_call(whole_kernel, out_shape=(pltpu.VMEM((512, B), f32), pltpu....  74.4 us

profile of v6, /device:TPU:1, one launch (start us, length us, event | category | flops | bytes accessed | tf_op | source)
XLA Modules:
  0.0 76.3 jit_solution(5014225638772376148)
XLA Ops:
  0.6 74.4 %shard_map.68 = (f32[512,256]{1,0:T(8,128)S(1)}, f32[256,1280]{1,0:T(8,128)S(1)}) custom-call(s32[1,256]{1,0:T(1,128)} %bitcast.4, s32[1,256]{1,0:T(1,128)} %bitcast.5, f32[2,1,256]{2,1,0:T(1,128)} %bitcast.3, bf16[512,512]{1,0:T(8,128)(2,1)} %features_hbm.1, f32[512,1024]{1,0:T(8,128)} %factor_hbm.1), custom_call_target="tpu_custom_call" | custom-call | tf_op jit(solution)/shard_map/pallas_call | solution.py:529
  75.1 1.3 %shard_map.69 = (f32[512,256]{1,0:T(8,128)}, f32[256,1280]{1,0:T(8,128)}) custom-call(f32[512,256]{1,0:T(8,128)S(1)} %get-tuple-element.4.columns, f32[256,1280]{1,0:T(8,128)S(1)} %get-tuple-element.5.gram), custom_call_target="tpu_custom_call" | custom-call | tf_op jit(solution)/shard_map/pallas_call | solution.py:591

commit v7 on v6

--- a/solution.py
+++ b/solution.py
@@ -279,10 +279,10 @@
     fx[c, 0, x] = total_x.astype(jnp.bfloat16)
     fh[c, x, 0] = total_h.astype(jnp.int16)
 
-    x_first = [copies.start(fx.at[c, 0, x], fx.at[c, 0, x], peer(**o)) for o in X_PEERS]
     z_first = [
         copies.start(fh.at[c, x, 0], fh.at[c, x, 7 - i], peer(**o)) for i, o in enumerate(Z_ORDER[::-1])
     ][::-1]
+    x_first = [copies.start(fx.at[c, 0, x], fx.at[c, 0, x], peer(**o)) for o in X_PEERS]
     for copy in x_first:
         copy.wait_recv()
     z_second = [

time: 76.5 us -> 76.3 us (level)
  no operation moved by 1% of the time
where the time goes in v7:
time: 76.3 us; the launch traced here: 76.2 us
  Pallas kernels  75.5 us (99%)
    pallas_call x1, Pallas kernels, run(): pl.pallas_call(whole_kernel, out_shape=(pltpu.VMEM((512, B), f32), pltpu....  74.3 us

profile of v7, /device:TPU:1, one launch (start us, length us, event | category | flops | bytes accessed | tf_op | source)
XLA Modules:
  0.0 76.2 jit_solution(2789380638840717905)
XLA Ops:
  0.6 74.3 %shard_map.68 = (f32[512,256]{1,0:T(8,128)S(1)}, f32[256,1280]{1,0:T(8,128)S(1)}) custom-call(s32[1,256]{1,0:T(1,128)} %bitcast.4, s32[1,256]{1,0:T(1,128)} %bitcast.5, f32[2,1,256]{2,1,0:T(1,128)} %bitcast.3, bf16[512,512]{1,0:T(8,128)(2,1)} %features_hbm.1, f32[512,1024]{1,0:T(8,128)} %factor_hbm.1), custom_call_target="tpu_custom_call" | custom-call | tf_op jit(solution)/shard_map/pallas_call | solution.py:529
  74.9 1.3 %shard_map.69 = (f32[512,256]{1,0:T(8,128)}, f32[256,1280]{1,0:T(8,128)}) custom-call(f32[512,256]{1,0:T(8,128)S(1)} %get-tuple-element.4.columns, f32[256,1280]{1,0:T(8,128)S(1)} %get-tuple-element.5.gram), custom_call_target="tpu_custom_call" | custom-call | tf_op jit(solution)/shard_map/pallas_call | solution.py:591
